TPU v7x, 256 devices: a whole 4x4x8 slice. The times are simulated.
256 devices in a mesh: batch: 16 (over z, y_hi), tile: 8 (over y_lo, x), cuts: 2 (over core).
Axes of the slice: x: 4, y: 4 (y_hi: 2, y_lo: 2; y = y_hi * 2 + y_lo), z: 8, core: 2. Of those that a mesh axis runs over, the one named last changes fastest.
Arguments:
- objects: float32 [2, 64, 2, 256, 256], P('cuts', 'tile'), may hold values from -5 to 5
- probe: float32 [4, 2, 256, 256], replicated, may hold values from -5 to 5
- measured: float32 [128, 256, 256], P(('batch', 'tile')), may hold values from 0 to 6
- send_list: int32 [16, 8, 8], P('batch', 'tile'), may hold values from 0 to 7
- corner_slot: int32 [128, 4], P(('batch', 'tile')), may hold values from 0 to 7
- offsets: int32 [128, 2], P(('batch', 'tile')), may hold values from 0 to 255
Outputs:
- new_objects: float32 [2, 64, 2, 256, 256], P('cuts', 'tile')
- new_probe: float32 [4, 2, 256, 256], P('cuts', None, 'tile')
Inputs may be any that keep to these rules, and one draw needn't show every extreme that they name: `send_list`: local tile indices of the owner. `corner_slot`: indices of the owner within the group.
All inputs are finite; a program needn't handle non-finite values.
Results may differ from a plain program's by a relative error of at most 0.0003.
Values sent between devices are 32-bit elements; how exact they have to be, the bound alone decides.
No kernel may reach another device: no remote copies, remote signals or barrier semaphores. Data moves between devices by JAX's collectives and lax.ppermute only.
A program may use at most 128 MiB of HBM per device.

v0:
```python
from functools import partial
import math

import jax
import jax.numpy as jnp
from jax import lax
from jax.sharding import PartitionSpec as P

HIGHEST_PRECISION = lax.Precision.HIGHEST
OBJECT_RATE = 0.02
PROBE_RATE = 0.05


def from_behind(block, axis, distance):
    devices = range(lax.axis_size(axis))
    route = [(i - distance, i) for i in devices if i - distance in devices]
    return lax.ppermute(block, axis, route)


def real_product(einsum_form, matrix, field_part):
    return jnp.einsum(einsum_form, matrix, field_part, precision=HIGHEST_PRECISION)


def one_side(matrix, field_pair, einsum_form):
    matrix_re, matrix_im = matrix
    field_re, field_im = field_pair
    return (
        real_product(einsum_form, matrix_re, field_re)
        - real_product(einsum_form, matrix_im, field_im),
        real_product(einsum_form, matrix_re, field_im)
        + real_product(einsum_form, matrix_im, field_re),
    )


def apply_both(matrix, field_pair):
    rows_done = one_side(matrix, field_pair, "jk,...kl->...jl")
    return one_side(matrix, rows_done, "lk,...jk->...jl")


def conjugate(matrix):
    return (matrix[0], -matrix[1])


def complex_times(left_side, right_side):
    return (
        left_side[0] * right_side[0] - left_side[1] * right_side[1],
        left_side[0] * right_side[1] + left_side[1] * right_side[0],
    )


def conj_times(left_side, right_side):
    return (
        left_side[0] * right_side[0] + left_side[1] * right_side[1],
        left_side[0] * right_side[1] - left_side[1] * right_side[0],
    )


def transform_tables(length):
    counter = jnp.arange(length, dtype=jnp.int32)
    turn_index = counter[:, None] * counter[None, :] % length
    angles = 2.0 * math.pi / length * turn_index.astype(jnp.float32)
    wave_re = jnp.cos(angles)
    wave_im = -jnp.sin(angles)
    signed = jnp.where(counter < length // 2, counter, counter - length)
    quadric = signed * signed % (2 * length)
    chirp_angle = math.pi / length * quadric.astype(jnp.float32)
    chirp_re = jnp.cos(chirp_angle)
    chirp_im = -jnp.sin(chirp_angle)
    scaled_re = wave_re * chirp_re[None, :] + wave_im * chirp_im[None, :]
    scaled_im = wave_re * chirp_im[None, :] - wave_im * chirp_re[None, :]
    dot_high = partial(jnp.dot, precision=HIGHEST_PRECISION)
    fresnel = (
        (dot_high(scaled_re, wave_re) - dot_high(scaled_im, wave_im)) / length,
        (dot_high(scaled_re, wave_im) + dot_high(scaled_im, wave_re)) / length,
    )
    unitary = 1.0 / math.sqrt(length)
    return (fresnel, (wave_re * unitary, wave_im * unitary))


def cut_window(region_one, start_cell, length):
    zero_index = jnp.zeros((), jnp.int32)
    return lax.dynamic_slice(
        region_one, (zero_index, start_cell[0], start_cell[1]), (2, length, length)
    )


def place_window(grad_one, start_cell, length):
    zero_index = jnp.zeros((), jnp.int32)
    zero_region = jnp.zeros((2, 2 * length, 2 * length), jnp.float32)
    return lax.dynamic_update_slice(
        zero_region, grad_one, (zero_index, start_cell[0], start_cell[1])
    )


def local(objects, probe, measured, send_list, corner_slot, offsets):
    length = probe.shape[-1]
    mode_count = probe.shape[0]
    half_modes = mode_count // 2
    local_count = measured.shape[0]
    groups = lax.axis_size("tile")
    row_block = length // groups
    slice_index = lax.axis_index("cuts")
    first_slice = slice_index == 0
    fresnel, farfield = transform_tables(length)
    probe_field = (probe[:, 0], probe[:, 1])
    owned_tiles = objects[0]
    pick_list = send_list[0, 0]
    outgoing = jnp.take(owned_tiles, pick_list, axis=0)
    arrived = lax.all_to_all(outgoing, "tile", split_axis=0, concat_axis=0, tiled=True)
    corners = jnp.take(arrived, corner_slot.reshape(-1), axis=0)
    region = corners.reshape(local_count, 2, 2, 2, length, length).transpose(0, 3, 1, 4, 2, 5)
    region = region.reshape(local_count, 2, 2 * length, 2 * length)
    patches = jax.vmap(partial(cut_window, length=length))(region, offsets)

    def forward_part(patch_pair):
        own_patch = (patch_pair[:, 0], patch_pair[:, 1])
        lit_field = complex_times(
            (probe_field[0][None], probe_field[1][None]),
            (own_patch[0][:, None], own_patch[1][:, None]),
        )
        spread = apply_both(fresnel, lit_field)
        return jnp.stack(
            [
                jnp.concatenate([spread[0], own_patch[0][:, None]], axis=1),
                jnp.concatenate([spread[1], own_patch[1][:, None]], axis=1),
            ]
        )

    def middle_part(wave_field, patch_pair, intensity_data):
        spread = (wave_field[0, :, :mode_count], wave_field[1, :, :mode_count])
        earlier = (wave_field[0, :, mode_count][:, None], wave_field[1, :, mode_count][:, None])
        own_patch = (patch_pair[:, 0][:, None], patch_pair[:, 1][:, None])
        exit_wave = complex_times(own_patch, spread)
        far_wave = apply_both(farfield, exit_wave)
        intensity = jnp.sum(far_wave[0] * far_wave[0] + far_wave[1] * far_wave[1], axis=1)
        residual = intensity - intensity_data
        weighted = (residual[:, None] * far_wave[0], residual[:, None] * far_wave[1])
        returned = apply_both(conjugate(farfield), weighted)
        second_terms = conj_times(spread, returned)
        grad_second = jnp.stack(
            [jnp.sum(second_terms[0], axis=1), jnp.sum(second_terms[1], axis=1)], axis=1
        )
        incoming = conj_times(own_patch, returned)
        upper_modes = (incoming[0][:, half_modes:], incoming[1][:, half_modes:])
        spread_back = apply_both(conjugate(fresnel), upper_modes)
        probe_upper = (probe_field[0][None, half_modes:], probe_field[1][None, half_modes:])
        first_terms = conj_times(probe_upper, spread_back)
        part_first = (jnp.sum(first_terms[0], axis=1), jnp.sum(first_terms[1], axis=1))
        probe_terms = conj_times(earlier, spread_back)
        probe_second = jnp.stack(
            [jnp.sum(probe_terms[0], axis=0), jnp.sum(probe_terms[1], axis=0)], axis=1
        )
        back_field = jnp.stack(
            [
                jnp.concatenate([incoming[0][:, :half_modes], part_first[0][:, None]], axis=1),
                jnp.concatenate([incoming[1][:, :half_modes], part_first[1][:, None]], axis=1),
            ]
        )
        return (back_field, grad_second, probe_second)

    def closing_part(back_field, patch_pair):
        lower_modes = (back_field[0, :, :half_modes], back_field[1, :, :half_modes])
        carried = (back_field[0, :, half_modes], back_field[1, :, half_modes])
        own_patch = (patch_pair[:, 0][:, None], patch_pair[:, 1][:, None])
        spread_back = apply_both(conjugate(fresnel), lower_modes)
        probe_lower = (probe_field[0][None, :half_modes], probe_field[1][None, :half_modes])
        first_terms = conj_times(probe_lower, spread_back)
        grad_first = jnp.stack(
            [
                jnp.sum(first_terms[0], axis=1) + carried[0],
                jnp.sum(first_terms[1], axis=1) + carried[1],
            ],
            axis=1,
        )
        probe_terms = conj_times(own_patch, spread_back)
        probe_first = jnp.stack(
            [jnp.sum(probe_terms[0], axis=0), jnp.sum(probe_terms[1], axis=0)], axis=1
        )
        return (grad_first, probe_first)

    def handle(patch_pair, intensity_data):
        position_count = patch_pair.shape[0]
        wave_field = lax.cond(
            first_slice,
            lambda: forward_part(patch_pair),
            lambda: jnp.zeros((2, position_count, mode_count + 1, length, length), jnp.float32),
        )
        wave_field = from_behind(wave_field, "cuts", 1)
        empty_result = lambda: (
            jnp.zeros((2, position_count, half_modes + 1, length, length), jnp.float32),
            jnp.zeros((position_count, 2, length, length), jnp.float32),
            jnp.zeros((half_modes, 2, length, length), jnp.float32),
        )
        back_field, grad_second, probe_second = lax.cond(
            first_slice, empty_result, lambda: middle_part(wave_field, patch_pair, intensity_data)
        )
        back_field = from_behind(back_field, "cuts", -1)
        return lax.cond(
            first_slice,
            lambda: closing_part(back_field, patch_pair),
            lambda: (grad_second, probe_second),
        )

    patch_grads, probe_term = handle(patches, measured)
    region_grads = jax.vmap(partial(place_window, length=length))(patch_grads, offsets)
    corner_grads = region_grads.reshape(local_count, 2, 2, length, 2, length).transpose(
        0, 2, 4, 1, 3, 5
    )
    corner_grads = corner_grads.reshape(local_count * 4, 2, length, length)
    slot_onehot = (
        corner_slot.reshape(-1)[None, :] == jnp.arange(groups, dtype=jnp.int32)[:, None]
    ).astype(jnp.float32)
    slot_grads = jnp.einsum("sk,kcyx->csyx", slot_onehot, corner_grads, precision=HIGHEST_PRECISION)
    probe_blocks = probe_term.reshape(half_modes * 2, groups, row_block, length)
    returned_grads, probe_pieces = (
        lax.all_to_all(slot_grads, "tile", split_axis=1, concat_axis=1, tiled=True),
        lax.all_to_all(probe_blocks, "tile", split_axis=1, concat_axis=1, tiled=True),
    )
    probe_rows = jnp.sum(probe_pieces, axis=1).reshape(half_modes, 2, row_block, length)
    tile_count = owned_tiles.shape[0]
    owner_onehot = (pick_list[None, :] == jnp.arange(tile_count, dtype=jnp.int32)[:, None]).astype(
        jnp.float32
    )
    tile_term = jnp.einsum(
        "ts,csyx->tcyx", owner_onehot, returned_grads, precision=HIGHEST_PRECISION
    )
    tile_total, probe_total = lax.psum((tile_term, probe_rows), "batch")
    new_objects = objects - OBJECT_RATE * tile_total[None]
    zero_index = jnp.zeros((), jnp.int32)
    mode_start = slice_index * half_modes
    row_start = lax.axis_index("tile") * row_block
    own_probe = lax.dynamic_slice(
        probe, (mode_start, zero_index, row_start, zero_index), (half_modes, 2, row_block, length)
    )
    position_total = local_count * lax.axis_size("batch") * groups
    new_probe = own_probe - PROBE_RATE / math.sqrt(position_total) * probe_total
    return (new_objects, new_probe)


def solution(mesh):
    in_specs = (
        P("cuts", "tile", None, None, None),
        P(),
        P(("batch", "tile"), None, None),
        P("batch", "tile", None),
        P(("batch", "tile"), None),
        P(("batch", "tile"), None),
    )
    out_specs = (P("cuts", "tile", None, None, None), P("cuts", None, "tile", None))
    return jax.shard_map(local, mesh=mesh, in_specs=in_specs, out_specs=out_specs, check_vma=False)
```

profile of v0, /device:TPU:2, one launch (start us, length us, event | category | flops | bytes accessed | tf_op | source)
XLA Modules:
  0.0 510.0 jit_solution(17351352646285451839)
XLA Ops:
  8.5 5.0 gather_fusion
  13.5 4.7 broadcast_select_fusion
  18.2 6.8 %all-to-all-start = ((f32[8,2,256,256]{3,2,1,0:T(8,128)}), f32[8,2,256,256]{3,2,1,0:T(8,128)}, u32[]{:S(2)}, u32[]{:S(2)}) async-start(f32[8,2,256,256]{3,2,1,0:T(8,128)} %broadcast_select_fusion), calls=%async_computation | async-start | bytes 8388608 | tf_op jit(solution)/shard_map/all_to_all | solution.py:109
  39.2 41.6 %all-to-all-done = f32[8,2,256,256]{3,2,1,0:T(8,128)} async-done(((f32[8,2,256,256]{3,2,1,0:T(8,128)}), f32[8,2,256,256]{3,2,1,0:T(8,128)}, u32[]{:S(2)}, u32[]{:S(2)}) %all-to-all-start) | async-done | bytes 4194336 | tf_op jit(solution)/shard_map/all_to_all | solution.py:109
  80.8 2.9 gather_fusion.1
  83.7 3.3 fusion.170
  87.0 4.0 reshape.611
  93.1 16.9 %conditional.3 = (f32[2,1,5,256,256]{4,3,2,1,0:T(8,128)S(1)}) conditional(s32[]{:T(128)} %convert_element_type.72, () %tuple.39, (f32[4,1,256,256]{3,2,0,1:T(8,128)S(1)}, f32[1,2,256,256]{3,2,1,0:T(8,128)}, f32[4,1,256,256]{3,2,0,1:T(8,128)}, f32[256,256]{1,0:T(8,128)S(1)}, f32[256,256]{1,0:T(8,128)S(1)}) %tuple.107), branch_computations={%region_1.2_spmd, %region_2.3_spmd} | conditional | flops 6447955968 | bytes 47710244 | solution.py:183
  113.9 3.5 collective-permute-done
  117.5 9.3 %conditional.4 = (f32[2,1,3,256,256]{4,3,2,1,0:T(8,128)S(1)}, f32[1,2,256,256]{3,2,1,0:T(8,128)}, f32[2,2,256,256]{3,2,0,1:T(8,128)}) conditional(s32[]{:T(128)} %convert_element_type.72, (f32[1,2,256,256]{3,2,1,0:T(8,128)}, f32[2,1,5,256,256]{4,3,2,1,0:T(8,128)S(1)}, f32[256,256]{1,0:T(8,128)S(1)}, f32[256,256]{1,0:T(8,128)S(1)}, ...), branch_computations={%region_3.9_spmd, %region_9.10_spmd} | conditional | flops 16121987072 | bytes 99614832 | solution.py:194
  129.7 37.4 %collective-permute-done.1 = f32[2,1,3,256,256]{3,4,2,1,0:T(8,128)S(1)} collective-permute-done((f32[2,1,3,256,256]{3,4,2,1,0:T(8,128)}, f32[2,1,3,256,256]{3,4,2,1,0:T(8,128)S(1)}, u32[]{:S(2)}, u32[]{:S(2)}) %collective-permute-start.1) | collective-permute-done | bytes 1572896 | tf_op jit(solution)/shard_map/ppermute | solution.py:17
  167.1 14.3 %conditional.5 = (f32[2,2,256,256]{3,2,0,1:T(8,128)}, f32[1,2,256,256]{3,2,1,0:T(8,128)}) conditional(s32[]{:T(128)} %convert_element_type.72, (f32[1,2,256,256]{3,2,1,0:T(8,128)}, f32[2,2,256,256]{3,2,0,1:T(8,128)}) %tuple.43, (f32[4,256,256]{2,1,0:T(8,128)}, f32[2,1,3,256,256]{3,4,2,1,0:T(8,128)S(1)}, f32[256,256]{1,0:T(8,128)S(1)}, ...), branch_computations={%region_10.11_spmd, %region_11.14_spmd} | conditional | flops 3224240128 | bytes 34078848 | solution.py:198
  173.7 2.9 add_reduce_fusion.2
  183.8 7.5 %all-to-all-start.2 = ((f32[4,8,32,256]{3,2,0,1:T(8,128)}), f32[4,8,32,256]{3,2,0,1:T(8,128)}, u32[]{:S(2)}, u32[]{:S(2)}) async-start(f32[4,8,32,256]{3,2,0,1:T(8,128)} %copy.194), calls=%async_computation.2 | async-start | bytes 2097152 | tf_op jit(solution)/shard_map/all_to_all | solution.py:217
  192.1 2.7 and_reduce_fusion
  197.2 12.0 %scatter.4 = f32[1,2,512,512]{3,2,1,0:T(8,128)S(1)} dynamic-update-slice(f32[1,2,512,512]{3,2,1,0:T(8,128)S(1)} %broadcast_in_dim.38, f32[1,2,256,256]{3,2,1,0:T(8,128)S(1)} %copy.187, s32[]{:T(128)} %constant.120.clone.1, s32[]{:T(128)} %constant.120.clone.1, s32[]{:T(128)} %bitcast.131, s32[]{:T(128)} %bitcast.132) | dynamic-update-slice | bytes 1048580 | tf_op jit(solution)/shard_map/vmap(vmap())/scatter | solution.py:90
  213.3 3.3 convolution_bitcast_fusion
  216.6 3.3 copy.190
  219.9 4.6 all-to-all-start.1
  226.8 37.1 %all-to-all-done.1 = f32[2,8,256,256]{3,2,0,1:T(8,128)} async-done(((f32[2,8,256,256]{3,2,0,1:T(8,128)}), f32[2,8,256,256]{3,2,0,1:T(8,128)}, u32[]{:S(2)}, u32[]{:S(2)}) %all-to-all-start.1) | async-done | bytes 4194336 | tf_op jit(solution)/shard_map/all_to_all | solution.py:216
  263.8 8.4 %fusion.167 = f32[8,2,256,256]{3,0,2,1:T(8,128)} fusion(f32[2,8,256,256]{3,2,0,1:T(8,128)} %all-to-all-done.1, s32[8]{0:T(128)S(1)} %bitcast.397), kind=kOutput, calls=%fused_computation.228 | convolution fusion | flops 100663360 | bytes 8388640 | tf_op jit(solution)/shard_map/ts,csyx->tcyx/dot_general | solution.py:224
  272.3 219.6 %all-reduce.3.cloned.1.call-done = (f32[8,2,256,256]{3,0,2,1:T(8,128)}, f32[2,2,32,256]{3,2,1,0:T(8,128)}) async-done(((f32[8,2,256,256]{3,0,2,1:T(8,128)}, f32[2,2,32,256]{3,2,1,0:T(8,128)}), (f32[8,2,256,256]{3,0,2,1:T(8,128)}, f32[2,2,32,256]{3,2,1,0:T(8,128)})) %all-reduce.3.cloned.1.call-update) | async-done | bytes 4325392 | tf_op jit(solution)/shard_map/psum | solution.py:227
  491.9 6.1 %bitcast_subtract_fusion.1 = f32[1,8,2,256,256]{4,1,3,2,0:T(8,128)S(1)} fusion(f32[1,8,2,256,256]{4,3,2,1,0:T(8,128)} %param.14, f32[8,2,256,256]{3,0,2,1:T(8,128)} %get-tuple-element.221), kind=kLoop, calls=%fused_computation.227 | loop fusion | flops 2097152 | bytes 12582912 | tf_op jit(solution)/shard_map/sub | solution.py:228
  498.0 3.3 copy.195
  (96 shorter events, 63.3 us)
Async XLA Ops:
  18.2 6.8 %copy-start.13 = (s32[1,2]{1,0:T(1,128)S(1)}, s32[1,2]{1,0:T(1,128)}, u32[]{:S(2)}) copy-start(s32[1,2]{1,0:T(1,128)} %param.19) | copy-start | bytes 28
  18.2 10.7 %copy-start.14 = (s32[1,4]{1,0:T(1,128)S(1)}, s32[1,4]{1,0:T(1,128)}, u32[]{:S(2)}) copy-start(s32[1,4]{1,0:T(1,128)} %param.18) | copy-start | bytes 52
  18.2 62.6 %all-to-all-start = ((f32[8,2,256,256]{3,2,1,0:T(8,128)}), f32[8,2,256,256]{3,2,1,0:T(8,128)}, u32[]{:S(2)}, u32[]{:S(2)}) async-start(f32[8,2,256,256]{3,2,1,0:T(8,128)} %broadcast_select_fusion), calls=%async_computation | async-start | bytes 8388608 | tf_op jit(solution)/shard_map/all_to_all | solution.py:109
  34.1 2.9 copy-start.6
  87.0 6.1 %copy-start.4 = (f32[4,1,256,256]{3,2,0,1:T(8,128)S(1)}, f32[4,1,256,256]{3,2,0,1:T(8,128)}, u32[]{:S(2)}) copy-start(f32[4,1,256,256]{3,2,0,1:T(8,128)} %get-tuple-element.255) | copy-start | bytes 3145732
  107.4 1.9 copy-start.9
  109.9 1.5 copy-start.5
  111.4 6.0 %collective-permute-start = (f32[2,1,5,256,256]{4,3,2,1,0:T(8,128)}, f32[2,1,5,256,256]{4,3,2,1,0:T(8,128)S(1)}, u32[]{:S(2)}, u32[]{:S(2)}) collective-permute-start(f32[2,1,5,256,256]{4,3,2,1,0:T(8,128)} %copy-done.5), channel_id=1, source_target_pairs={{0,1},{2,3},{4,5},{6,7},{8,9},{10,11},{12,13},{14,15},{16,17},{18,... | collective-permute-start | bytes 7864328 | tf_op jit(solution)/shard_map/ppermute | solution.py:17
  126.8 40.3 %copy-start = (f32[4,256,256]{2,1,0:T(8,128)S(1)}, f32[4,256,256]{2,1,0:T(8,128)}, u32[]{:S(2)}) copy-start(f32[4,256,256]{2,1,0:T(8,128)} %get-tuple-element.253) | copy-start | bytes 3145732
  128.4 38.6 %collective-permute-start.1 = (f32[2,1,3,256,256]{3,4,2,1,0:T(8,128)}, f32[2,1,3,256,256]{3,4,2,1,0:T(8,128)S(1)}, u32[]{:S(2)}, u32[]{:S(2)}) collective-permute-start(f32[2,1,3,256,256]{3,4,2,1,0:T(8,128)} %copy.185), channel_id=1, source_target_pairs={{1,0},{3,2},{5,4},{7,6},{9,8},{11,10},{13,12},{15,14},{17,16},{19,... | collective-permute-start | bytes 4718600 | tf_op jit(solution)/shard_map/ppermute | solution.py:17
  170.6 3.1 copy-start.3
  176.7 1.6 copy-start.10
  178.3 2.0 copy-start.7
  178.3 2.0 copy-start.8
  182.7 8.7 %copy-start.16 = (s32[1,3]{1,0:T(1,128)S(1)}, s32[1,3]{1,0:T(1,128)}, u32[]{:S(2)}) copy-start(s32[1,3]{1,0:T(1,128)} %constant.124.clone.1) | copy-start | bytes 40
  182.7 9.4 %copy-start.17 = (s32[4]{0:T(128)S(1)}, s32[4]{0:T(128)}, u32[]{:S(2)}) copy-start(s32[4]{0:T(128)} %constant.125.clone.1) | copy-start | bytes 52
  183.8 36.0 %all-to-all-start.2 = ((f32[4,8,32,256]{3,2,0,1:T(8,128)}), f32[4,8,32,256]{3,2,0,1:T(8,128)}, u32[]{:S(2)}, u32[]{:S(2)}) async-start(f32[4,8,32,256]{3,2,0,1:T(8,128)} %copy.194), calls=%async_computation.2 | async-start | bytes 2097152 | tf_op jit(solution)/shard_map/all_to_all | solution.py:217
  219.9 44.0 %copy-start.15 = (s32[1,1,8]{2,1,0:T(1,128)S(1)}, s32[1,1,8]{2,1,0:T(1,128)}, u32[]{:S(2)}) copy-start(s32[1,1,8]{2,1,0:T(1,128)} %param.17) | copy-start | bytes 100
  219.9 44.0 %all-to-all-start.1 = ((f32[2,8,256,256]{3,2,0,1:T(8,128)}), f32[2,8,256,256]{3,2,0,1:T(8,128)}, u32[]{:S(2)}, u32[]{:S(2)}) async-start(f32[2,8,256,256]{3,2,0,1:T(8,128)} %copy.190), calls=%async_computation.1 | async-start | bytes 8388608 | tf_op jit(solution)/shard_map/all_to_all | solution.py:216
  224.5 267.4 %all-reduce.3.cloned.1.call-start = ((), (), s32[]{:S(2)}) async-start(), calls=%async_computation.3 | async-start | bytes 8650752 | tf_op jit(solution)/shard_map/psum | solution.py:227
  498.0 3.3 copy-start.12
Sparse Core Ops, SparseCore 0:
  272.4 219.4 all-reduce.2
where the time goes:
time: 519 us; the launch traced here: 510 us
  waiting for transfers between devices  339 us (65%)
  local copies, waits for them, and re-layouts  56.8 us (11%)
  matrix products  37.6 us (7%)
  other arithmetic  27.7 us (5%)
  starting transfers between devices  22 us (4%)
  between operations  18.7 us (4%)
  loops' own time  8.14 us (2%)
    psum x1, waiting for transfers between devices, local(): tile_total, probe_total = lax.psum((tile_term, probe_rows), 'batch')  220 us
    all_to_all x1, waiting for transfers between devices, local(): lax.all_to_all(outgoing, 'tile', split_axis=0, concat_axis=0, tiled=True)  41.6 us
    ppermute x2, waiting for transfers between devices, from_behind(): return lax.ppermute(block, axis, route)  40.9 us
    all_to_all x1, waiting for transfers between devices, local(): lax.all_to_all(slot_grads, 'tile', split_axis=1, concat_axis=1, tiled=True)  37.1 us
    dot_general x16, matrix products, real_product(): jnp.einsum(einsum_form, matrix, field_part, precision=HIGHEST_PRECISION)  20.1 us
    scatter x1, local copies, waits for them, and re-layouts, place_window(): lax.dynamic_update_slice(zero_region, grad_one, (zero_index, start_cell[0...  12 us
  transfers between devices with their start and end apart: 6, of which 5 were waited for; matrix products, arithmetic and copies ran while one was open for 8% of the time, Pallas kernels for 0%

commit v1 on v0

v1 whole, which is shorter than its diff:
```python
from functools import partial
import math

import jax
import jax.numpy as jnp
from jax import lax
from jax.experimental import pallas as pl
from jax.experimental.pallas import tpu as pltpu
from jax.sharding import PartitionSpec as P
import ml_dtypes
import numpy as np

OBJECT_RATE = 0.02
PROBE_RATE = 0.05
LANES = 128
BIG = pltpu.CompilerParams(vmem_limit_bytes=56 * 1024 * 1024)
F32 = jnp.float32
BF16 = jnp.bfloat16


def halves(matrix):
    upper = matrix.astype(ml_dtypes.bfloat16)
    lower = (matrix - upper.astype(np.float64)).astype(ml_dtypes.bfloat16)
    return upper, lower


def block_matrices(matrix):
    re, im = matrix.real, matrix.imag
    left = np.block([[re, -im], [im, re]])
    right = np.block([[re, im], [-im, re]])
    return halves(left) + halves(right)


def transform_tables(length):
    counter = np.arange(length)
    wave = np.exp(-2j * math.pi / length * (counter[:, None] * counter[None, :] % length))
    signed = np.where(counter < length // 2, counter, counter - length)
    chirp = np.exp(-1j * math.pi / length * (signed * signed % (2 * length)))
    fresnel = (np.conj(wave) * chirp[None, :]) @ wave / length
    return block_matrices(fresnel) + block_matrices(wave / math.sqrt(length))


def split(value):
    upper = value.astype(BF16)
    lower = (value - upper.astype(F32)).astype(BF16)
    return upper, lower


def dot(a, b):
    return jnp.dot(a, b, preferred_element_type=F32)


def two_sided(re, im, left, right):
    n = re.shape[0]
    upper, lower = split(jnp.concatenate([re, im], axis=0))
    rows = dot(left[0][...], upper) + dot(left[0][...], lower) + dot(left[1][...], upper)
    upper, lower = split(jnp.concatenate([rows[:n], rows[n:]], axis=1))
    both = dot(upper, right[0][...]) + dot(lower, right[0][...]) + dot(upper, right[1][...])
    return both[:, :n], both[:, n:]


def gather_kernel(pick_ref, tile_ref, out_ref):
    n = tile_ref.shape[-1]
    for part in range(2):
        for side in range(n // LANES):
            panel = part * (n // LANES) + side
            out_ref[0, panel * n : (panel + 1) * n, :] = tile_ref[0, part, :, side * LANES : (side + 1) * LANES]


def gather_tiles(pick, tiles):
    count = pick.shape[0]
    n = tiles.shape[-1]
    rows = 2 * n * (n // LANES)
    return pl.pallas_call(
        gather_kernel,
        grid_spec=pltpu.PrefetchScalarGridSpec(
            num_scalar_prefetch=1,
            grid=(count,),
            in_specs=[pl.BlockSpec((1, 2, n, n), lambda i, pick: (pick[i], 0, 0, 0))],
            out_specs=pl.BlockSpec((1, rows, LANES), lambda i, pick: (i, 0, 0)),
        ),
        out_shape=jax.ShapeDtypeStruct((count, rows, LANES), F32),
        compiler_params=BIG,
        name="gather_tiles",
    )(pick, tiles)


def select_kernel(n, info_ref, c0_ref, c1_ref, c2_ref, c3_ref, out_ref):
    y0, x0 = info_ref[4], info_ref[5]
    sides = n // LANES
    for panel in range(2 * sides):
        rows = slice(panel * n, (panel + 1) * n)
        u = lax.broadcasted_iota(jnp.int32, (n, LANES), 0)
        v = lax.broadcasted_iota(jnp.int32, (n, LANES), 1) + (panel % sides) * LANES
        low, right = u < y0, v < x0
        upper = jnp.where(right, c1_ref[0, rows, :], c0_ref[0, rows, :])
        lower = jnp.where(right, c3_ref[0, rows, :], c2_ref[0, rows, :])
        out_ref[rows, :] = jnp.where(low, lower, upper)


def select_corners(info, arrived, n):
    rows = arrived.shape[1]
    spec = lambda k: pl.BlockSpec((1, rows, LANES), lambda i, info: (info[k], 0, 0))
    return pl.pallas_call(
        partial(select_kernel, n),
        grid_spec=pltpu.PrefetchScalarGridSpec(
            num_scalar_prefetch=1,
            grid=(1,),
            in_specs=[spec(0), spec(1), spec(2), spec(3)],
            out_specs=pl.BlockSpec((rows, LANES), lambda i, info: (0, 0)),
        ),
        out_shape=jax.ShapeDtypeStruct((rows, LANES), F32),
        compiler_params=BIG,
        name="select_corners",
    )(info, arrived, arrived, arrived, arrived)


def wave_kernel(
    info_ref, own_ref, other_ref, probe_ref, data_ref, meta_ref,
    pl0, pl1, pr0, pr1, fl0, fl1, fr0, fr1,
    out_ref, spread, far, rolled, weight, total, q0, q1,
):
    n = data_ref.shape[-1]
    modes = probe_ref.shape[0]
    half = modes // 2
    sides = n // LANES
    groups = out_ref.shape[0]
    batches = 2 * sides * n // 8 // groups
    y0, x0, cut = info_ref[4], info_ref[5], info_ref[6]
    y_back, x_back = lax.rem(n - y0, n), lax.rem(n - x0, n)
    first = cut == 0
    prop_left, prop_right = (pl0, pl1), (pr0, pr1)
    far_left, far_right = (fl0, fl1), (fr0, fr1)
    for panel in range(2 * sides):
        part, side = panel // sides, panel % sides
        own = own_ref[panel * n : (panel + 1) * n, :]
        other = other_ref[panel * n : (panel + 1) * n, :]
        lanes = slice(side * LANES, (side + 1) * LANES)
        q0[part, :, lanes] = jnp.where(first, own, other)
        q1[part, :, lanes] = jnp.where(first, other, own)
    weight[...] = -data_ref[0]

    def forward(m, carry):
        pre = pltpu.roll(pltpu.roll(probe_ref[m, 0], y0, 0), x0, 1)
        pim = pltpu.roll(pltpu.roll(probe_ref[m, 1], y0, 0), x0, 1)
        rolled[m, 0], rolled[m, 1] = pre, pim
        re, im = two_sided(
            pre * q0[0] - pim * q0[1], pre * q0[1] + pim * q0[0], prop_left, prop_right
        )
        spread[m, 0], spread[m, 1] = re, im
        re, im = two_sided(q1[0] * re - q1[1] * im, q1[0] * im + q1[1] * re, far_left, far_right)
        far[m, 0], far[m, 1] = re, im
        weight[...] += re * re + im * im
        return carry

    lax.fori_loop(0, modes, forward, 0)
    total[...] = jnp.zeros_like(total)

    def backward(m, carry):
        cre, cim = two_sided(
            weight[...] * far[m, 0], weight[...] * far[m, 1], far_right, far_left
        )

        @pl.when(jnp.logical_not(first))
        def _():
            sre, sim = spread[m, 0], spread[m, 1]
            total[0] += sre * cre + sim * cim
            total[1] += sre * cim - sim * cre

        @pl.when(jnp.logical_or(first, m >= half))
        def _():
            zre, zim = two_sided(
                q1[0] * cre + q1[1] * cim, q1[0] * cim - q1[1] * cre, prop_right, prop_left
            )

            @pl.when(first)
            def _():
                pre, pim = rolled[m, 0], rolled[m, 1]
                total[0] += pre * zre + pim * zim
                total[1] += pre * zim - pim * zre

            @pl.when(lax.div(m, half) == cut)
            def _():
                slot = lax.rem(m, half)
                parts = (q0[0] * zre + q0[1] * zim, q0[0] * zim - q0[1] * zre)
                for part in range(2):
                    term = pltpu.roll(pltpu.roll(parts[part], y_back, 0), x_back, 1)
                    rows = n // groups
                    for side in range(sides):
                        base = batches * 8 + (slot * 2 + part) * sides * rows + side * rows
                        base = pl.multiple_of(base, 8)
                        for t in range(groups):
                            out_ref[t, pl.ds(base, rows), :] = term[
                                t * rows : (t + 1) * rows, side * LANES : (side + 1) * LANES
                            ]

        return carry

    lax.fori_loop(0, modes, backward, 0)
    for j in range(2 * sides * n // 8):
        b, t = j // groups, j % groups
        panel, row = divmod(j * 8, n)
        part, side = panel // sides, panel % sides
        out_ref[t, b * 8 : (b + 1) * 8, :] = total[
            part, row : row + 8, side * LANES : (side + 1) * LANES
        ]
    rows = out_ref.shape[1]
    for t in range(groups):
        out_ref[t, rows - 8 : rows, :] = meta_ref[...]


def wave_terms(info, own, other, probe, measured, meta, groups):
    n = probe.shape[-1]
    modes = probe.shape[0]
    tables = [jnp.asarray(table) for table in transform_tables(n)]
    g_rows = 2 * n * n // LANES // groups
    rows = g_rows + modes * n * n // LANES // groups + 8
    whole = pl.BlockSpec(memory_space=pltpu.VMEM)
    return pl.pallas_call(
        wave_kernel,
        in_specs=[pl.BlockSpec(memory_space=pltpu.SMEM)] + [whole] * (5 + len(tables)),
        out_specs=whole,
        out_shape=jax.ShapeDtypeStruct((groups, rows, LANES), F32),
        scratch_shapes=[
            pltpu.VMEM((modes, 2, n, n), F32),
            pltpu.VMEM((modes, 2, n, n), F32),
            pltpu.VMEM((modes, 2, n, n), F32),
            pltpu.VMEM((n, n), F32),
            pltpu.VMEM((2, n, n), F32),
            pltpu.VMEM((2, n, n), F32),
            pltpu.VMEM((2, n, n), F32),
        ],
        compiler_params=BIG,
        name="wave_terms",
    )(info, own, other, probe, measured, meta, *tables)


def regroup_kernel(g_tiles, p_rows, in_ref, out_ref):
    groups = in_ref.shape[0]
    batches = out_ref.shape[0]
    last = in_ref.shape[1] - 8
    for b in range(batches):
        for t in range(groups):
            out_ref[b, t * 8 : (t + 1) * 8, :] = in_ref[t, b * 8 : (b + 1) * 8, :]
        base = g_tiles * 8 + b * p_rows
        term = in_ref[0, base : base + p_rows, :]
        for t in range(1, groups):
            term = term + in_ref[t, base : base + p_rows, :]
        out_ref[b, groups * 8 : groups * 8 + p_rows, :] = term
        for t in range(groups):
            row = groups * 8 + p_rows + t
            out_ref[b, row : row + 1, :] = in_ref[t, last : last + 1, :]


def regroup(pieces, batches):
    groups, rows, _ = pieces.shape
    p_rows = (rows - 8 - batches * 8) // batches
    whole = pl.BlockSpec(memory_space=pltpu.VMEM)
    return pl.pallas_call(
        partial(regroup_kernel, batches, p_rows),
        in_specs=[whole],
        out_specs=whole,
        out_shape=jax.ShapeDtypeStruct((batches, groups * 8 + p_rows + 8, LANES), F32),
        compiler_params=BIG,
        name="regroup",
    )(pieces)


def reduce_kernel(n, groups, p_rows, info_ref, table_ref, in_ref, out_ref, acc):
    batches = in_ref.shape[0]
    tiles = acc.shape[1] // 8
    sides = n // LANES
    place = info_ref[7]
    panel, row = lax.div(place * 8, n), lax.rem(place * 8, n)
    u = lax.broadcasted_iota(jnp.int32, (8, LANES), 0) + row
    v = lax.broadcasted_iota(jnp.int32, (8, LANES), 1) + lax.rem(panel, sides) * LANES
    acc[...] = jnp.zeros_like(acc)

    def one_batch(b, carry):
        for t in range(groups):
            at = (b * groups + t) * 8
            value = in_ref[b, t * 8 : (t + 1) * 8, :]
            low, right = u < table_ref[at + 4], v < table_ref[at + 5]
            lower, upper = jnp.where(low, value, 0.0), jnp.where(low, 0.0, value)
            corners = (
                jnp.where(right, 0.0, upper),
                jnp.where(right, upper, 0.0),
                jnp.where(right, 0.0, lower),
                jnp.where(right, lower, 0.0),
            )
            for k in range(4):
                where = pl.ds(pl.multiple_of(table_ref[at + k] * 8, 8), 8)
                acc[k, where, :] += corners[k]
        return carry

    lax.fori_loop(0, batches, one_batch, 0)
    per_owner = tiles // groups * 8
    probe_sum = in_ref[0, groups * 8 : groups * 8 + p_rows, :]
    for b in range(1, batches):
        probe_sum = probe_sum + in_ref[b, groups * 8 : groups * 8 + p_rows, :]
    for o in range(groups):
        rows = slice(o * per_owner, (o + 1) * per_owner)
        summed = (acc[0, rows, :] + acc[1, rows, :]) + (acc[2, rows, :] + acc[3, rows, :])
        for copy in range(2):
            out_ref[copy * groups + o, :per_owner, :] = summed
            out_ref[copy * groups + o, per_owner:, :] = probe_sum


def reduce_positions(info, table, pieces, n, groups, tiles):
    p_rows = pieces.shape[1] - groups * 8 - 8
    whole = pl.BlockSpec(memory_space=pltpu.VMEM)
    smem = pl.BlockSpec(memory_space=pltpu.SMEM)
    return pl.pallas_call(
        partial(reduce_kernel, n, groups, p_rows),
        in_specs=[smem, smem, whole],
        out_specs=whole,
        out_shape=jax.ShapeDtypeStruct((2 * groups, tiles * 8 // groups + p_rows, LANES), F32),
        scratch_shapes=[pltpu.VMEM((4, tiles * 8, LANES), F32)],
        compiler_params=BIG,
        name="reduce_positions",
    )(info, table, pieces)


def pack_kernel(p_rows, place_ref, in_ref, out_ref):
    groups = in_ref.shape[0] // 2
    t_rows = in_ref.shape[1] - p_rows
    for h in range(2):
        for t in range(groups):
            out_ref[h, t * t_rows : (t + 1) * t_rows, :] = in_ref[h * groups + t, :t_rows, :]
        out_ref[h, groups * t_rows :, :] = in_ref[h * groups + place_ref[0], t_rows:, :]


def pack(place, pieces, p_rows):
    groups = pieces.shape[0] // 2
    rows = groups * (pieces.shape[1] - p_rows) + p_rows
    whole = pl.BlockSpec(memory_space=pltpu.VMEM)
    return pl.pallas_call(
        partial(pack_kernel, p_rows),
        in_specs=[pl.BlockSpec(memory_space=pltpu.SMEM), whole],
        out_specs=whole,
        out_shape=jax.ShapeDtypeStruct((2, rows, LANES), F32),
        compiler_params=BIG,
        name="pack",
    )(place, pieces)


def update_kernel(groups, probe_rate, where_ref, *refs):
    tile_ref, grad_ref, probe_ref, pgrad_ref = refs[:4]
    new_tile_ref, new_probe_ref = refs[-2:]
    count = tile_ref.shape[0]
    for t in range(groups):
        for l in range(count):
            at = (t * count + l) * 8
            rows = slice(t * 8, (t + 1) * 8)
            new_tile_ref[l, 0, rows, :] = (
                tile_ref[l, 0, rows, :] - OBJECT_RATE * grad_ref[at : at + 8, :]
            )
    new_probe_ref[0, 0] = probe_ref[0, 0] - probe_rate * pgrad_ref[...]


def update(where, tiles, chunk, probe, state, groups, p_rows, probe_rate, half):
    count, _, n, _ = tiles.shape
    rows = groups * 8
    row_blocks = n // rows
    sides = n // LANES
    strips = n // groups // p_rows
    main = chunk.shape[0] - p_rows

    def tile_at(i, w):
        panel = w[0] // row_blocks
        return (0, panel // sides, lax.rem(w[0], row_blocks), lax.rem(panel, sides))

    def own_probe_at(w):
        strip = lax.rem(w[0], strips)
        panel = w[0] // strips
        return panel // sides // 2, lax.rem(panel // sides, 2), strip, lax.rem(panel, sides)

    def new_probe_at(i, w):
        return own_probe_at(w)

    def probe_at(i, w):
        m, part, strip, side = own_probe_at(w)
        return m + w[1] * half, part, strip + w[2] * strips, side

    tile_spec = pl.BlockSpec((count, 1, rows, LANES), tile_at)
    in_specs = [
        tile_spec,
        pl.BlockSpec((main, LANES), lambda i, w: (0, 0)),
        pl.BlockSpec((1, 1, p_rows, LANES), probe_at),
        pl.BlockSpec((p_rows, LANES), lambda i, w: (main // p_rows, 0)),
    ]
    operands = [tiles, chunk, probe, chunk]
    aliases = {}
    if state is not None:
        in_specs += [pl.BlockSpec(memory_space=pl.ANY)] * 2
        operands += list(state)
        aliases = {5: 0, 6: 1}
    return pl.pallas_call(
        partial(update_kernel, groups, probe_rate),
        grid_spec=pltpu.PrefetchScalarGridSpec(
            num_scalar_prefetch=1,
            grid=(1,),
            in_specs=in_specs,
            out_specs=[tile_spec, pl.BlockSpec((1, 1, p_rows, LANES), new_probe_at)],
        ),
        out_shape=[
            jax.ShapeDtypeStruct(tiles.shape, F32),
            jax.ShapeDtypeStruct((half, 2, n // groups, n), F32),
        ],
        input_output_aliases=aliases,
        compiler_params=BIG,
        cost_estimate=pl.CostEstimate(
            flops=2 * main * LANES, bytes_accessed=12 * main * LANES, transcendentals=0
        ),
        name="update",
    )(where, *operands)


def local(objects, probe, measured, send_list, corner_slot, offsets):
    n = probe.shape[-1]
    half = probe.shape[0] // 2
    groups = lax.axis_size("tile")
    batches = lax.axis_size("batch")
    z_size = batches // 2
    cut = lax.axis_index("cuts")
    member = lax.axis_index("tile")
    batch = lax.axis_index("batch")
    tiles = objects[0]
    tile_count = tiles.shape[0]
    info = jnp.concatenate(
        [
            corner_slot.reshape(-1),
            offsets.reshape(-1),
            jnp.stack([cut, batch * groups + member]).astype(jnp.int32),
        ]
    )
    meta_row = jnp.concatenate(
        [send_list.reshape(-1), corner_slot.reshape(-1), offsets.reshape(-1)]
    ).astype(F32)
    meta = jnp.zeros((8, LANES), F32).at[0, : meta_row.shape[0]].set(meta_row)

    with jax.named_scope("fetch_tiles"):
        outgoing = gather_tiles(send_list.reshape(-1), tiles)
        arrived = lax.all_to_all(outgoing, "tile", split_axis=0, concat_axis=0, tiled=True)
        own = select_corners(info, arrived, n)
        other = lax.ppermute(own, "cuts", [(0, 1), (1, 0)])
    with jax.named_scope("waves"):
        pieces = wave_terms(info, own, other, probe, measured, meta, groups)
    with jax.named_scope("return_terms"):
        pieces = lax.all_to_all(pieces, "tile", split_axis=0, concat_axis=0, tiled=True)
        pieces = regroup(pieces, batches)
        pieces = lax.all_to_all(pieces, "batch", split_axis=0, concat_axis=0, tiled=True)
        last = pieces.shape[1] - 8
        notes = pieces[:, last:, : meta_row.shape[0]].astype(jnp.int32)
        lists, slots, starts = notes[..., :groups], notes[..., groups : groups + 4], notes[..., groups + 4 :]
        owners = jnp.arange(groups, dtype=jnp.int32)
        chosen = slots[:, None, :, :] == owners[None, :, None, None]
        sent = jnp.sum(jnp.where(chosen, lists[:, :, :, None], 0), axis=1)
        table = jnp.concatenate(
            [slots * tile_count + sent, starts, jnp.zeros_like(starts)], axis=-1
        ).reshape(-1)
        p_rows = last - groups * 8
        summed = reduce_positions(info, table, pieces, n, groups, groups * tile_count)
        planes = [
            [(z * 2 + h) * groups + t for h in range(2) for t in range(groups)]
            for z in range(z_size)
        ]
        summed = lax.all_to_all(
            summed, ("batch", "tile"), split_axis=0, concat_axis=0, axis_index_groups=planes, tiled=True
        )
        packed = pack(member.reshape(1).astype(jnp.int32), summed, p_rows)
    with jax.named_scope("spread_sums"):
        onward = [(i, (i + 2) % batches) for i in range(batches)]
        backward = [(i, (i - 2) % batches) for i in range(batches)]
        z = batch // 2
        rate = PROBE_RATE / math.sqrt(batches * groups * measured.shape[0])
        found = []
        ahead = [packed[0], packed[1]]
        behind = [packed[0], packed[1]]
        for h in range(2):
            found.append((z, h, packed[h]))
        for step in range(1, z_size // 2 + 1):
            final = step == z_size // 2
            for h in range(2):
                if not (final and h == 1):
                    ahead[h] = lax.ppermute(ahead[h], "batch", onward)
                    found.append((z - step, h, ahead[h]))
                if not (final and h == 0):
                    behind[h] = lax.ppermute(behind[h], "batch", backward)
                    found.append((z + step, h, behind[h]))
        state = None
        for place, h, chunk in found:
            row = lax.rem(place + z_size, z_size) * 2 + h
            where = jnp.stack([row, cut, member]).astype(jnp.int32)
            state = update(where, tiles, chunk, probe, state, groups, p_rows, rate, half)
    return (state[0][None], state[1])


def solution(mesh):
    in_specs = (
        P("cuts", "tile", None, None, None),
        P(),
        P(("batch", "tile"), None, None),
        P("batch", "tile", None),
        P(("batch", "tile"), None),
        P(("batch", "tile"), None),
    )
    out_specs = (P("cuts", "tile", None, None, None), P("cuts", None, "tile", None))
    return jax.shard_map(local, mesh=mesh, in_specs=in_specs, out_specs=out_specs, check_vma=False)
```

time: 519 us -> 273 us (0.53); the launches traced: 510 us -> 272 us
  waiting for transfers between devices: 339 us -> 94.7 us
  Pallas kernels: 0 us -> 93.8 us
  local copies, waits for them, and re-layouts: 56.8 us -> 5.34 us
  matrix products: 37.6 us -> 0 us
  blocking collectives: 0 us -> 24.8 us
  starting transfers between devices: 22 us -> 41.8 us
  between operations: 18.7 us -> 0.85 us
  other arithmetic: 27.7 us -> 10.4 us
  loops' own time: 8.14 us -> 0 us
    psum x1 -> x0, waiting for transfers between devices: 220 us -> none  [local(): tile_total, probe_total = lax.psum((tile_term, probe_rows), 'batch')]
    pallas_call x0 -> x22, Pallas kernels: none -> 93.8 us  [the longest x16 39.5 us: update(): pl.pallas_call(partial(update_kernel, groups, probe_rate), grid_spec=pltp...]
    dot_general x22 -> x0, matrix products: 37.6 us -> none  [the longest x16 20.1 us: real_product(): jnp.einsum(einsum_form, matrix, field_part, precision=HIGHEST_PRECISION)]
    ppermute x2 -> x15, waiting for transfers between devices: 40.9 us -> 11.4 us  [the longest x7 9.99 us: local(): ahead[h] = lax.ppermute(ahead[h], 'batch', onward)]
    all_to_all x0 -> x1, blocking collectives: none -> 24.8 us  [local(): lax.all_to_all(pieces, 'tile', split_axis=0, concat_axis=0, tiled=True)]
    ppermute x2 -> x15, starting transfers between devices: 2.73 us -> 19.4 us  [the longest x7 17 us: local(): behind[h] = lax.ppermute(behind[h], 'batch', backward)]
    all_to_all x1, waiting for transfers between devices: 41.6 us -> 57.1 us  [local(): lax.all_to_all(outgoing, 'tile', split_axis=0, concat_axis=0, tiled=True)]
    scatter x1, local copies, waits for them, and re-layouts: 12 us -> 0.6 us  [local(): meta = jnp.zeros((8, LANES), F32).at[0, :meta_row.shape[0]].set(meta_row)]
  transfers between devices with their start and end apart: 6 -> 18, of which waited for: 5 -> 7; matrix products, arithmetic and copies ran while one was open for 8% -> 4% of each run, Pallas kernels for 0% -> 14%
where the time goes in v1:
time: 273 us; the launch traced here: 272 us
  waiting for transfers between devices  94.7 us (35%)
  Pallas kernels  93.8 us (34%)
  starting transfers between devices  41.8 us (15%)
  blocking collectives  24.8 us (9%)
  other arithmetic  10.4 us (4%)
  local copies, waits for them, and re-layouts  5.34 us (2%)
    all_to_all x1, waiting for transfers between devices, local(): lax.all_to_all(outgoing, 'tile', split_axis=0, concat_axis=0, tiled=True)  57.1 us
    pallas_call x16, Pallas kernels, update(): pl.pallas_call(partial(update_kernel, groups, probe_rate), grid_spec=pltp...  39.5 us
    pallas_call x1, Pallas kernels, wave_terms(): pl.pallas_call(wave_kernel, in_specs=[pl.BlockSpec(memory_space=pltpu.SME...  35 us
    all_to_all x1, blocking collectives, local(): lax.all_to_all(pieces, 'tile', split_axis=0, concat_axis=0, tiled=True)  24.8 us
    all_to_all x1, waiting for transfers between devices, local(): lax.all_to_all(pieces, 'batch', split_axis=0, concat_axis=0, tiled=True)  18.4 us
    ppermute x7, starting transfers between devices, local(): behind[h] = lax.ppermute(behind[h], 'batch', backward)  17 us
    all_to_all x1, starting transfers between devices, local(): lax.all_to_all(pieces, 'batch', split_axis=0, concat_axis=0, tiled=True)  11.5 us
    ppermute x7, waiting for transfers between devices, local(): ahead[h] = lax.ppermute(ahead[h], 'batch', onward)  9.99 us
  transfers between devices with their start and end apart: 18, of which 7 were waited for; matrix products, arithmetic and copies ran while one was open for 4% of the time, Pallas kernels for 14%

profile of v1, /device:TPU:2, one launch (start us, length us, event | category | flops | bytes accessed | tf_op | source)
XLA Modules:
  0.0 271.6 jit_solution(4845543254055550681)
XLA Ops:
  0.6 7.6 %gather_tiles.1 = f32[8,1024,128]{2,1,0:T(8,128)} custom-call(s32[8]{0:T(128)} %bitcast.49, f32[8,2,256,256]{3,2,1,0:T(8,128)} %bitcast.30), custom_call_target="tpu_custom_call" | custom-call | tf_op jit(solution)/shard_map/fetch_tiles/gather_tiles/pallas_call | solution.py:74
  8.2 6.0 %all-to-all-start = ((f32[8,1024,128]{2,1,0:T(8,128)}), f32[8,1024,128]{2,1,0:T(8,128)}, u32[]{:S(2)}, u32[]{:S(2)}) async-start(f32[8,1024,128]{2,1,0:T(8,128)} %gather_tiles.1), calls=%async_computation | async-start | bytes 8388608 | tf_op jit(solution)/shard_map/fetch_tiles/all_to_all | solution.py:444
  15.0 57.1 %all-to-all-done.c0_ref.c1_ref.c2_ref.c3_ref = f32[8,1024,128]{2,1,0:T(8,128)} async-done(((f32[8,1024,128]{2,1,0:T(8,128)}), f32[8,1024,128]{2,1,0:T(8,128)}, u32[]{:S(2)}, u32[]{:S(2)}) %all-to-all-start) | async-done | bytes 4194336 | tf_op jit(solution)/shard_map/fetch_tiles/all_to_all | solution.py:444
  72.1 3.1 %select_corners.1.own_ref = f32[1024,128]{1,0:T(8,128)} custom-call(s32[8]{0:T(128)} %pad_add_fusion.info_ref, f32[8,1024,128]{2,1,0:T(8,128)} %all-to-all-done.c0_ref.c1_ref.c2_ref.c3_ref, f32[8,1024,128]{2,1,0:T(8,128)} %all-to-all-done.c0_ref.c1_ref.c2_ref.c3_ref, f32[8,1024,128]{2,1,0:T(8,128)} %all-to-all-done.c0_ref.c1_ref.c2_ref.c3_ref, ...), custom_call_target="tpu_custom_call" | custom-call | tf_op jit(solution)/shard_map/fetch_tiles/select_corners/pallas_call | solution.py:104
  78.0 35.0 %wave_terms.1 = f32[8,392,128]{2,1,0:T(8,128)} custom-call(s32[8]{0:T(128)} %pad_add_fusion.info_ref, f32[1024,128]{1,0:T(8,128)} %select_corners.1.own_ref, f32[1024,128]{1,0:T(8,128)} %copy-done.15, f32[4,2,256,256]{3,2,1,0:T(8,128)} %refs_2_.31, f32[1,256,256]{2,1,0:T(8,128)} %data_ref.1, f32[8,128]{1,0:T(8,128)} %scatter.4.meta_ref, ...), custom_call_target="tpu_custom_call" | custom-call | tf_op jit(solution)/shard_map/waves/wave_terms/pallas_call | solution.py:219
  113.0 24.8 %all_to_all.20.in_ref = f32[8,392,128]{2,1,0:T(8,128)} all-to-all(f32[8,392,128]{2,1,0:T(8,128)} %wave_terms.1), channel_id=1, replica_groups=mesh['batch'=16,'tile'=8,'cuts'=2] {'tile'}, dimensions={0} | all-to-all | bytes 3211264 | tf_op jit(solution)/shard_map/return_terms/all_to_all | solution.py:450
  140.2 11.5 %all-to-all-start.2 = ((f32[16,88,128]{2,1,0:T(8,128)}), f32[16,88,128]{2,1,0:T(8,128)S(1)}, u32[]{:S(2)}, u32[]{:S(2)}) async-start(f32[16,88,128]{2,1,0:T(8,128)} %regroup.1), calls=%async_computation.2 | async-start | bytes 1441792 | tf_op jit(solution)/shard_map/return_terms/all_to_all | solution.py:452
  151.8 18.4 %all-to-all-done.2.in_ref = f32[16,88,128]{2,1,0:T(8,128)S(1)} async-done(((f32[16,88,128]{2,1,0:T(8,128)}), f32[16,88,128]{2,1,0:T(8,128)S(1)}, u32[]{:S(2)}, u32[]{:S(2)}) %all-to-all-start.2) | async-done | bytes 720928 | tf_op jit(solution)/shard_map/return_terms/all_to_all | solution.py:452
  171.7 4.3 %reduce_positions.1 = f32[16,80,128]{2,1,0:T(8,128)} custom-call(s32[8]{0:T(128)} %pad_add_fusion.info_ref, s32[1024]{0:T(1024)} %reshape.81.table_ref, f32[16,88,128]{2,1,0:T(8,128)} %copy-done), custom_call_target="tpu_custom_call" | custom-call | tf_op jit(solution)/shard_map/return_terms/reduce_positions/pallas_call | solution.py:313
  176.0 4.8 %all-to-all-start.3 = ((f32[16,80,128]{2,1,0:T(8,128)}), f32[16,80,128]{2,1,0:T(8,128)S(1)}, u32[]{:S(2)}, u32[]{:S(2)}) async-start(f32[16,80,128]{2,1,0:T(8,128)} %reduce_positions.1), calls=%async_computation.3 | async-start | bytes 1310720 | tf_op jit(solution)/shard_map/return_terms/all_to_all | solution.py:468
  182.7 7.7 %all-to-all-done.3.in_ref = f32[16,80,128]{2,1,0:T(8,128)S(1)} async-done(((f32[16,80,128]{2,1,0:T(8,128)}), f32[16,80,128]{2,1,0:T(8,128)S(1)}, u32[]{:S(2)}, u32[]{:S(2)}) %all-to-all-start.3) | async-done | bytes 655392 | tf_op jit(solution)/shard_map/return_terms/all_to_all | solution.py:468
  194.3 3.2 %collective-permute-start.1 = (f32[528,128]{1,0:T(8,128)S(1)}, f32[528,128]{1,0:T(8,128)S(1)}, u32[]{:S(2)}, u32[]{:S(2)}) collective-permute-start(f32[528,128]{1,0:T(8,128)S(1)} %get-tuple-element.79.refs_1_.refs_3_), channel_id=1, source_target_pairs={{0,224},{16,240},{32,0},{48,16},{64,32},{80,48},{96,64},{112,80},{... | collective-permute-start | bytes 811016 | tf_op jit(solution)/shard_map/spread_sums/ppermute | solution.py:489
  201.5 3.3 %collective-permute-done.5.refs_1_.refs_3_ = f32[528,128]{1,0:T(8,128)S(1)} collective-permute-done((f32[528,128]{1,0:T(8,128)S(1)}, f32[528,128]{1,0:T(8,128)S(1)}, u32[]{:S(2)}, u32[]{:S(2)}) %collective-permute-start.5) | collective-permute-done | bytes 270368 | tf_op jit(solution)/shard_map/spread_sums/ppermute | solution.py:486
  204.8 3.2 %collective-permute-start.2 = (f32[528,128]{1,0:T(8,128)S(1)}, f32[528,128]{1,0:T(8,128)S(1)}, u32[]{:S(2)}, u32[]{:S(2)}) collective-permute-start(f32[528,128]{1,0:T(8,128)S(1)} %collective-permute-done.1.refs_1_.refs_3_), channel_id=1, source_target_pairs={{0,224},{16,240},{32,0},{48,16},{64,32},{80,48},{96,64},{112,80},{... | collective-permute-start | bytes 811016 | tf_op jit(solution)/shard_map/spread_sums/ppermute | solution.py:489
  212.2 4.2 %collective-permute-done.6.refs_1_.refs_3_ = f32[528,128]{1,0:T(8,128)S(1)} collective-permute-done((f32[528,128]{1,0:T(8,128)S(1)}, f32[528,128]{1,0:T(8,128)S(1)}, u32[]{:S(2)}, u32[]{:S(2)}) %collective-permute-start.6) | collective-permute-done | bytes 270368 | tf_op jit(solution)/shard_map/spread_sums/ppermute | solution.py:486
  216.7 2.9 %collective-permute-start.3 = (f32[528,128]{1,0:T(8,128)S(1)}, f32[528,128]{1,0:T(8,128)S(1)}, u32[]{:S(2)}, u32[]{:S(2)}) collective-permute-start(f32[528,128]{1,0:T(8,128)S(1)} %collective-permute-done.2.refs_1_.refs_3_), channel_id=1, source_target_pairs={{0,224},{16,240},{32,0},{48,16},{64,32},{80,48},{96,64},{112,80},{... | collective-permute-start | bytes 811016 | tf_op jit(solution)/shard_map/spread_sums/ppermute | solution.py:489
  223.7 2.5 collective-permute-done.7.refs_1_.refs_3_
  226.2 3.2 %collective-permute-start.4 = (f32[528,128]{1,0:T(8,128)S(1)}, f32[528,128]{1,0:T(8,128)S(1)}, u32[]{:S(2)}, u32[]{:S(2)}) collective-permute-start(f32[528,128]{1,0:T(8,128)S(1)} %collective-permute-done.3.refs_1_.refs_3_), channel_id=1, source_target_pairs={{0,224},{16,240},{32,0},{48,16},{64,32},{80,48},{96,64},{112,80},{... | collective-permute-start | bytes 811016 | tf_op jit(solution)/shard_map/spread_sums/ppermute | solution.py:489
  233.8 2.5 update.17
  236.3 2.5 update.18
  251.1 2.5 update.24
  258.5 2.5 update.27
  261.0 2.5 update.28
  265.9 2.5 update.30
  (104 shorter events, 53.0 us)
Async XLA Ops:
  8.2 63.8 %all-to-all-start = ((f32[8,1024,128]{2,1,0:T(8,128)}), f32[8,1024,128]{2,1,0:T(8,128)}, u32[]{:S(2)}, u32[]{:S(2)}) async-start(f32[8,1024,128]{2,1,0:T(8,128)} %gather_tiles.1), calls=%async_computation | async-start | bytes 8388608 | tf_op jit(solution)/shard_map/fetch_tiles/all_to_all | solution.py:444
  15.0 60.2 %copy-start.16 = (s32[1,1,8]{2,1,0:T(1,128)S(1)}, s32[1,1,8]{2,1,0:T(1,128)}, u32[]{:S(2)}) copy-start(s32[1,1,8]{2,1,0:T(1,128)} %param.19) | copy-start | bytes 100
  75.1 2.1 collective-permute-start
  140.2 30.0 %all-to-all-start.2 = ((f32[16,88,128]{2,1,0:T(8,128)}), f32[16,88,128]{2,1,0:T(8,128)S(1)}, u32[]{:S(2)}, u32[]{:S(2)}) async-start(f32[16,88,128]{2,1,0:T(8,128)} %regroup.1), calls=%async_computation.2 | async-start | bytes 1441792 | tf_op jit(solution)/shard_map/return_terms/all_to_all | solution.py:452
  176.0 14.4 %all-to-all-start.3 = ((f32[16,80,128]{2,1,0:T(8,128)}), f32[16,80,128]{2,1,0:T(8,128)S(1)}, u32[]{:S(2)}, u32[]{:S(2)}) async-start(f32[16,80,128]{2,1,0:T(8,128)} %reduce_positions.1), calls=%async_computation.3 | async-start | bytes 1310720 | tf_op jit(solution)/shard_map/return_terms/all_to_all | solution.py:468
  194.2 37.1 %copy-start.2 = (f32[528,128]{1,0:T(8,128)}, f32[528,128]{1,0:T(8,128)S(1)}, u32[]{:S(2)}) copy-start(f32[528,128]{1,0:T(8,128)S(1)} %get-tuple-element.78.refs_1_.refs_3_) | copy-start | bytes 811012
  194.2 39.5 %copy-start.3 = (f32[528,128]{1,0:T(8,128)}, f32[528,128]{1,0:T(8,128)S(1)}, u32[]{:S(2)}) copy-start(f32[528,128]{1,0:T(8,128)S(1)} %get-tuple-element.79.refs_1_.refs_3_) | copy-start | bytes 811012
  194.2 10.6 %collective-permute-start.5 = (f32[528,128]{1,0:T(8,128)S(1)}, f32[528,128]{1,0:T(8,128)S(1)}, u32[]{:S(2)}, u32[]{:S(2)}) collective-permute-start(f32[528,128]{1,0:T(8,128)S(1)} %get-tuple-element.78.refs_1_.refs_3_), channel_id=1, source_target_pairs={{0,32},{16,48},{32,64},{48,80},{64,96},{80,112},{96,128},{112,144}... | collective-permute-start | bytes 811016 | tf_op jit(solution)/shard_map/spread_sums/ppermute | solution.py:486
  194.3 10.5 %collective-permute-start.1 = (f32[528,128]{1,0:T(8,128)S(1)}, f32[528,128]{1,0:T(8,128)S(1)}, u32[]{:S(2)}, u32[]{:S(2)}) collective-permute-start(f32[528,128]{1,0:T(8,128)S(1)} %get-tuple-element.79.refs_1_.refs_3_), channel_id=1, source_target_pairs={{0,224},{16,240},{32,0},{48,16},{64,32},{80,48},{96,64},{112,80},{... | collective-permute-start | bytes 811016 | tf_op jit(solution)/shard_map/spread_sums/ppermute | solution.py:489
  199.5 10.4 %collective-permute-start.12 = (f32[528,128]{1,0:T(8,128)S(1)}, f32[528,128]{1,0:T(8,128)S(1)}, u32[]{:S(2)}, u32[]{:S(2)}) collective-permute-start(f32[528,128]{1,0:T(8,128)S(1)} %get-tuple-element.78.refs_1_.refs_3_), channel_id=1, source_target_pairs={{0,224},{16,240},{32,0},{48,16},{64,32},{80,48},{96,64},{112,80},{... | collective-permute-start | bytes 811016 | tf_op jit(solution)/shard_map/spread_sums/ppermute | solution.py:489
  199.5 12.7 %collective-permute-start.9 = (f32[528,128]{1,0:T(8,128)S(1)}, f32[528,128]{1,0:T(8,128)S(1)}, u32[]{:S(2)}, u32[]{:S(2)}) collective-permute-start(f32[528,128]{1,0:T(8,128)S(1)} %get-tuple-element.79.refs_1_.refs_3_), channel_id=1, source_target_pairs={{0,32},{16,48},{32,64},{48,80},{64,96},{80,112},{96,128},{112,144}... | collective-permute-start | bytes 811016 | tf_op jit(solution)/shard_map/spread_sums/ppermute | solution.py:486
  204.8 31.4 %copy-start.5 = (f32[528,128]{1,0:T(8,128)}, f32[528,128]{1,0:T(8,128)S(1)}, u32[]{:S(2)}) copy-start(f32[528,128]{1,0:T(8,128)S(1)} %collective-permute-done.5.refs_1_.refs_3_) | copy-start | bytes 811012
  204.8 11.6 %collective-permute-start.6 = (f32[528,128]{1,0:T(8,128)S(1)}, f32[528,128]{1,0:T(8,128)S(1)}, u32[]{:S(2)}, u32[]{:S(2)}) collective-permute-start(f32[528,128]{1,0:T(8,128)S(1)} %collective-permute-done.5.refs_1_.refs_3_), channel_id=1, source_target_pairs={{0,32},{16,48},{32,64},{48,80},{64,96},{80,112},{96,128},{112,144}... | collective-permute-start | bytes 811016 | tf_op jit(solution)/shard_map/spread_sums/ppermute | solution.py:486
  204.8 31.4 %copy-start.4 = (f32[528,128]{1,0:T(8,128)}, f32[528,128]{1,0:T(8,128)S(1)}, u32[]{:S(2)}) copy-start(f32[528,128]{1,0:T(8,128)S(1)} %collective-permute-done.1.refs_1_.refs_3_) | copy-start | bytes 811012
  204.8 11.9 %collective-permute-start.2 = (f32[528,128]{1,0:T(8,128)S(1)}, f32[528,128]{1,0:T(8,128)S(1)}, u32[]{:S(2)}, u32[]{:S(2)}) collective-permute-start(f32[528,128]{1,0:T(8,128)S(1)} %collective-permute-done.1.refs_1_.refs_3_), channel_id=1, source_target_pairs={{0,224},{16,240},{32,0},{48,16},{64,32},{80,48},{96,64},{112,80},{... | collective-permute-start | bytes 811016 | tf_op jit(solution)/shard_map/spread_sums/ppermute | solution.py:489
  209.9 26.3 %copy-start.11 = (f32[528,128]{1,0:T(8,128)}, f32[528,128]{1,0:T(8,128)S(1)}, u32[]{:S(2)}) copy-start(f32[528,128]{1,0:T(8,128)S(1)} %collective-permute-done.12.refs_1_.refs_3_) | copy-start | bytes 811012
  209.9 11.7 %collective-permute-start.13 = (f32[528,128]{1,0:T(8,128)S(1)}, f32[528,128]{1,0:T(8,128)S(1)}, u32[]{:S(2)}, u32[]{:S(2)}) collective-permute-start(f32[528,128]{1,0:T(8,128)S(1)} %collective-permute-done.12.refs_1_.refs_3_), channel_id=1, source_target_pairs={{0,224},{16,240},{32,0},{48,16},{64,32},{80,48},{96,64},{112,80},{... | collective-permute-start | bytes 811016 | tf_op jit(solution)/shard_map/spread_sums/ppermute | solution.py:489
  212.2 11.4 %collective-permute-start.10 = (f32[528,128]{1,0:T(8,128)S(1)}, f32[528,128]{1,0:T(8,128)S(1)}, u32[]{:S(2)}, u32[]{:S(2)}) collective-permute-start(f32[528,128]{1,0:T(8,128)S(1)} %collective-permute-done.9.refs_1_.refs_3_), channel_id=1, source_target_pairs={{0,32},{16,48},{32,64},{48,80},{64,96},{80,112},{96,128},{112,144}... | collective-permute-start | bytes 811016 | tf_op jit(solution)/shard_map/spread_sums/ppermute | solution.py:486
  216.4 9.8 %collective-permute-start.7 = (f32[528,128]{1,0:T(8,128)S(1)}, f32[528,128]{1,0:T(8,128)S(1)}, u32[]{:S(2)}, u32[]{:S(2)}) collective-permute-start(f32[528,128]{1,0:T(8,128)S(1)} %collective-permute-done.6.refs_1_.refs_3_), channel_id=1, source_target_pairs={{0,32},{16,48},{32,64},{48,80},{64,96},{80,112},{96,128},{112,144}... | collective-permute-start | bytes 811016 | tf_op jit(solution)/shard_map/spread_sums/ppermute | solution.py:486
  216.7 9.5 %collective-permute-start.3 = (f32[528,128]{1,0:T(8,128)S(1)}, f32[528,128]{1,0:T(8,128)S(1)}, u32[]{:S(2)}, u32[]{:S(2)}) collective-permute-start(f32[528,128]{1,0:T(8,128)S(1)} %collective-permute-done.2.refs_1_.refs_3_), channel_id=1, source_target_pairs={{0,224},{16,240},{32,0},{48,16},{64,32},{80,48},{96,64},{112,80},{... | collective-permute-start | bytes 811016 | tf_op jit(solution)/shard_map/spread_sums/ppermute | solution.py:489
  221.6 37.0 %collective-permute-start.14 = (f32[528,128]{1,0:T(8,128)S(1)}, f32[528,128]{1,0:T(8,128)}, u32[]{:S(2)}, u32[]{:S(2)}) collective-permute-start(f32[528,128]{1,0:T(8,128)S(1)} %collective-permute-done.13.refs_1_.refs_3_), channel_id=1, source_target_pairs={{0,224},{16,240},{32,0},{48,16},{64,32},{80,48},{96,64},{112,80},{... | collective-permute-start | bytes 811016 | tf_op jit(solution)/shard_map/spread_sums/ppermute | solution.py:489
  223.7 37.3 %collective-permute-start.11 = (f32[528,128]{1,0:T(8,128)S(1)}, f32[528,128]{1,0:T(8,128)}, u32[]{:S(2)}, u32[]{:S(2)}) collective-permute-start(f32[528,128]{1,0:T(8,128)S(1)} %collective-permute-done.10.refs_1_.refs_3_), channel_id=1, source_target_pairs={{0,32},{16,48},{32,64},{48,80},{64,96},{80,112},{96,128},{112,144}... | collective-permute-start | bytes 811016 | tf_op jit(solution)/shard_map/spread_sums/ppermute | solution.py:486
  226.2 39.8 %collective-permute-start.8 = (f32[528,128]{1,0:T(8,128)S(1)}, f32[528,128]{1,0:T(8,128)}, u32[]{:S(2)}, u32[]{:S(2)}) collective-permute-start(f32[528,128]{1,0:T(8,128)S(1)} %collective-permute-done.7.refs_1_.refs_3_), channel_id=1, source_target_pairs={{0,32},{16,48},{32,64},{48,80},{64,96},{80,112},{96,128},{112,144}... | collective-permute-start | bytes 811016 | tf_op jit(solution)/shard_map/spread_sums/ppermute | solution.py:486
  226.2 42.2 %collective-permute-start.4 = (f32[528,128]{1,0:T(8,128)S(1)}, f32[528,128]{1,0:T(8,128)S(1)}, u32[]{:S(2)}, u32[]{:S(2)}) collective-permute-start(f32[528,128]{1,0:T(8,128)S(1)} %collective-permute-done.3.refs_1_.refs_3_), channel_id=1, source_target_pairs={{0,224},{16,240},{32,0},{48,16},{64,32},{80,48},{96,64},{112,80},{... | collective-permute-start | bytes 811016 | tf_op jit(solution)/shard_map/spread_sums/ppermute | solution.py:489
  (13 other events, 126.9 us)

commit v2 on v1

--- a/solution.py
+++ b/solution.py
@@ -50,13 +50,28 @@
     return jnp.dot(a, b, preferred_element_type=F32)
 
 
-def two_sided(re, im, left, right):
-    n = re.shape[0]
-    upper, lower = split(jnp.concatenate([re, im], axis=0))
+def two_sided(fields, left, right):
+    n = fields[0][0].shape[0]
+    parts = [jnp.concatenate([field[part] for field in fields], axis=1) for part in range(2)]
+    upper, lower = split(jnp.concatenate(parts, axis=0))
     rows = dot(left[0][...], upper) + dot(left[0][...], lower) + dot(left[1][...], upper)
-    upper, lower = split(jnp.concatenate([rows[:n], rows[n:]], axis=1))
+    stacked = [
+        jnp.concatenate([rows[:n, i * n : (i + 1) * n], rows[n:, i * n : (i + 1) * n]], axis=1)
+        for i in range(len(fields))
+    ]
+    upper, lower = split(jnp.concatenate(stacked, axis=0))
     both = dot(upper, right[0][...]) + dot(lower, right[0][...]) + dot(upper, right[1][...])
-    return both[:, :n], both[:, n:]
+    return [
+        (both[i * n : (i + 1) * n, :n], both[i * n : (i + 1) * n, n:]) for i in range(len(fields))
+    ]
+
+
+def times(a, b):
+    return a[0] * b[0] - a[1] * b[1], a[0] * b[1] + a[1] * b[0]
+
+
+def conj_times(a, b):
+    return a[0] * b[0] + a[1] * b[1], a[0] * b[1] - a[1] * b[0]
 
 
 def gather_kernel(pick_ref, tile_ref, out_ref):
@@ -139,64 +154,65 @@
         q0[part, :, lanes] = jnp.where(first, own, other)
         q1[part, :, lanes] = jnp.where(first, other, own)
     weight[...] = -data_ref[0]
-
-    def forward(m, carry):
-        pre = pltpu.roll(pltpu.roll(probe_ref[m, 0], y0, 0), x0, 1)
-        pim = pltpu.roll(pltpu.roll(probe_ref[m, 1], y0, 0), x0, 1)
-        rolled[m, 0], rolled[m, 1] = pre, pim
-        re, im = two_sided(
-            pre * q0[0] - pim * q0[1], pre * q0[1] + pim * q0[0], prop_left, prop_right
-        )
-        spread[m, 0], spread[m, 1] = re, im
-        re, im = two_sided(q1[0] * re - q1[1] * im, q1[0] * im + q1[1] * re, far_left, far_right)
-        far[m, 0], far[m, 1] = re, im
-        weight[...] += re * re + im * im
-        return carry
-
-    lax.fori_loop(0, modes, forward, 0)
+    for m in range(modes):
+        for part in range(2):
+            rolled[m, part] = pltpu.roll(pltpu.roll(probe_ref[m, part], y0, 0), x0, 1)
+    pairs = [range(i * half, (i + 1) * half) for i in range(2)]
+
+    for pair in pairs:
+        lit = [times((rolled[m, 0], rolled[m, 1]), (q0[0], q0[1])) for m in pair]
+        waves = two_sided(lit, prop_left, prop_right)
+        exits = []
+        for m, wave in zip(pair, waves):
+            spread[m, 0], spread[m, 1] = wave
+            exits.append(times((q1[0], q1[1]), wave))
+        waves = two_sided(exits, far_left, far_right)
+        power = jnp.zeros((n, n), F32)
+        for m, wave in zip(pair, waves):
+            far[m, 0], far[m, 1] = wave
+            power = power + (wave[0] * wave[0] + wave[1] * wave[1])
+        weight[...] += power
+
     total[...] = jnp.zeros_like(total)
-
-    def backward(m, carry):
-        cre, cim = two_sided(
-            weight[...] * far[m, 0], weight[...] * far[m, 1], far_right, far_left
-        )
+    for place, pair in enumerate(pairs):
+        weighted = [(weight[...] * far[m, 0], weight[...] * far[m, 1]) for m in pair]
+        chis = two_sided(weighted, far_right, far_left)
+        for m, chi in zip(pair, chis):
+            far[m, 0], far[m, 1] = chi
 
         @pl.when(jnp.logical_not(first))
         def _():
-            sre, sim = spread[m, 0], spread[m, 1]
-            total[0] += sre * cre + sim * cim
-            total[1] += sre * cim - sim * cre
-
-        @pl.when(jnp.logical_or(first, m >= half))
+            for m in pair:
+                term = conj_times((spread[m, 0], spread[m, 1]), (far[m, 0], far[m, 1]))
+                total[0] += term[0]
+                total[1] += term[1]
+
+        @pl.when(jnp.logical_or(first, place == 1))
         def _():
-            zre, zim = two_sided(
-                q1[0] * cre + q1[1] * cim, q1[0] * cim - q1[1] * cre, prop_right, prop_left
-            )
+            backs = [conj_times((q1[0], q1[1]), (far[m, 0], far[m, 1])) for m in pair]
+            zetas = two_sided(backs, prop_right, prop_left)
 
             @pl.when(first)
             def _():
-                pre, pim = rolled[m, 0], rolled[m, 1]
-                total[0] += pre * zre + pim * zim
-                total[1] += pre * zim - pim * zre
-
-            @pl.when(lax.div(m, half) == cut)
+                for m, zeta in zip(pair, zetas):
+                    term = conj_times((rolled[m, 0], rolled[m, 1]), zeta)
+                    total[0] += term[0]
+                    total[1] += term[1]
+
+            @pl.when(place == cut)
             def _():
-                slot = lax.rem(m, half)
-                parts = (q0[0] * zre + q0[1] * zim, q0[0] * zim - q0[1] * zre)
-                for part in range(2):
-                    term = pltpu.roll(pltpu.roll(parts[part], y_back, 0), x_back, 1)
-                    rows = n // groups
-                    for side in range(sides):
-                        base = batches * 8 + (slot * 2 + part) * sides * rows + side * rows
-                        base = pl.multiple_of(base, 8)
-                        for t in range(groups):
-                            out_ref[t, pl.ds(base, rows), :] = term[
-                                t * rows : (t + 1) * rows, side * LANES : (side + 1) * LANES
-                            ]
-
-        return carry
-
-    lax.fori_loop(0, modes, backward, 0)
+                rows = n // groups
+                for slot, zeta in enumerate(zetas):
+                    parts = conj_times((q0[0], q0[1]), zeta)
+                    for part in range(2):
+                        term = pltpu.roll(pltpu.roll(parts[part], y_back, 0), x_back, 1)
+                        for side in range(sides):
+                            base = batches * 8 + ((slot * 2 + part) * sides + side) * rows
+                            for t in range(groups):
+                                out_ref[t, base : base + rows, :] = term[
+                                    t * rows : (t + 1) * rows, side * LANES : (side + 1) * LANES
+                                ]
+
     for j in range(2 * sides * n // 8):
         b, t = j // groups, j % groups
         panel, row = divmod(j * 8, n)
@@ -321,13 +337,15 @@
     )(info, table, pieces)
 
 
-def pack_kernel(p_rows, place_ref, in_ref, out_ref):
+def pack_kernel(p_rows, place_ref, in_ref, *out_refs):
     groups = in_ref.shape[0] // 2
     t_rows = in_ref.shape[1] - p_rows
     for h in range(2):
         for t in range(groups):
-            out_ref[h, t * t_rows : (t + 1) * t_rows, :] = in_ref[h * groups + t, :t_rows, :]
-        out_ref[h, groups * t_rows :, :] = in_ref[h * groups + place_ref[0], t_rows:, :]
+            for l in range(t_rows // 8):
+                at = (l * groups + t) * 8
+                out_refs[h][at : at + 8, :] = in_ref[h * groups + t, l * 8 : (l + 1) * 8, :]
+        out_refs[h][groups * t_rows :, :] = in_ref[h * groups + place_ref[0], t_rows:, :]
 
 
 def pack(place, pieces, p_rows):
@@ -337,83 +355,72 @@
     return pl.pallas_call(
         partial(pack_kernel, p_rows),
         in_specs=[pl.BlockSpec(memory_space=pltpu.SMEM), whole],
-        out_specs=whole,
-        out_shape=jax.ShapeDtypeStruct((2, rows, LANES), F32),
+        out_specs=[whole, whole],
+        out_shape=[jax.ShapeDtypeStruct((rows, LANES), F32)] * 2,
         compiler_params=BIG,
         name="pack",
     )(place, pieces)
 
 
-def update_kernel(groups, probe_rate, where_ref, *refs):
-    tile_ref, grad_ref, probe_ref, pgrad_ref = refs[:4]
-    new_tile_ref, new_probe_ref = refs[-2:]
-    count = tile_ref.shape[0]
-    for t in range(groups):
-        for l in range(count):
-            at = (t * count + l) * 8
-            rows = slice(t * 8, (t + 1) * 8)
-            new_tile_ref[l, 0, rows, :] = (
-                tile_ref[l, 0, rows, :] - OBJECT_RATE * grad_ref[at : at + 8, :]
+def update_kernel(probe_rate, half, p_rows, where_ref, tile_ref, probe_ref, *refs):
+    count = (len(refs) - 2) // 2
+    grads, pgrads = refs[:count], refs[count : 2 * count]
+    new_tile_ref, new_probe_ref = refs[2 * count :]
+    n = tile_ref.shape[-1]
+    sides = n // LANES
+    rows = grads[0].shape[0]
+    row_blocks = n // rows
+    for i in range(count):
+        batch = where_ref[i]
+        panel = lax.div(batch, row_blocks)
+        part, side = lax.div(panel, sides), lax.rem(panel, sides)
+        at = pl.ds(pl.multiple_of(lax.rem(batch, row_blocks) * rows, rows), rows)
+        lanes = pl.ds(pl.multiple_of(side * LANES, LANES), LANES)
+        new_tile_ref[0, part, at, lanes] = (
+            tile_ref[0, part, at, lanes] - OBJECT_RATE * grads[i][...]
+        )
+
+    @pl.when(pl.program_id(0) == 0)
+    def _():
+        strips = new_probe_ref.shape[2] // p_rows
+        for i in range(count):
+            batch = where_ref[i]
+            panel = lax.div(batch, strips)
+            field, side = lax.div(panel, sides), lax.rem(panel, sides)
+            m, part = lax.div(field, 2), lax.rem(field, 2)
+            at = pl.ds(pl.multiple_of(lax.rem(batch, strips) * p_rows, p_rows), p_rows)
+            lanes = pl.ds(pl.multiple_of(side * LANES, LANES), LANES)
+            new_probe_ref[m, part, at, lanes] = (
+                probe_ref[m, part, at, lanes] - probe_rate * pgrads[i][...]
             )
-    new_probe_ref[0, 0] = probe_ref[0, 0] - probe_rate * pgrad_ref[...]
-
-
-def update(where, tiles, chunk, probe, state, groups, p_rows, probe_rate, half):
+
+
+def update(where, tiles, probe, chunks, groups, p_rows, probe_rate):
     count, _, n, _ = tiles.shape
+    half = probe.shape[0] // 2
+    batches = len(chunks)
     rows = groups * 8
-    row_blocks = n // rows
-    sides = n // LANES
-    strips = n // groups // p_rows
-    main = chunk.shape[0] - p_rows
-
-    def tile_at(i, w):
-        panel = w[0] // row_blocks
-        return (0, panel // sides, lax.rem(w[0], row_blocks), lax.rem(panel, sides))
-
-    def own_probe_at(w):
-        strip = lax.rem(w[0], strips)
-        panel = w[0] // strips
-        return panel // sides // 2, lax.rem(panel // sides, 2), strip, lax.rem(panel, sides)
-
-    def new_probe_at(i, w):
-        return own_probe_at(w)
-
-    def probe_at(i, w):
-        m, part, strip, side = own_probe_at(w)
-        return m + w[1] * half, part, strip + w[2] * strips, side
-
-    tile_spec = pl.BlockSpec((count, 1, rows, LANES), tile_at)
+    main = chunks[0].shape[0] - p_rows
+    tile_spec = pl.BlockSpec((1, 2, n, n), lambda i, w: (i, 0, 0, 0))
+    probe_shape = (half, 2, n // groups, n)
     in_specs = [
         tile_spec,
-        pl.BlockSpec((main, LANES), lambda i, w: (0, 0)),
-        pl.BlockSpec((1, 1, p_rows, LANES), probe_at),
-        pl.BlockSpec((p_rows, LANES), lambda i, w: (main // p_rows, 0)),
+        pl.BlockSpec(probe_shape, lambda i, w: (w[batches], 0, w[batches + 1], 0)),
     ]
-    operands = [tiles, chunk, probe, chunk]
-    aliases = {}
-    if state is not None:
-        in_specs += [pl.BlockSpec(memory_space=pl.ANY)] * 2
-        operands += list(state)
-        aliases = {5: 0, 6: 1}
-    return pl.pallas_call(
-        partial(update_kernel, groups, probe_rate),
+    in_specs += [pl.BlockSpec((rows, LANES), lambda i, w: (i, 0))] * batches
+    in_specs += [pl.BlockSpec((p_rows, LANES), lambda i, w: (main // p_rows, 0))] * batches
+    return pl.pallas_call(
+        partial(update_kernel, probe_rate, half, p_rows),
         grid_spec=pltpu.PrefetchScalarGridSpec(
             num_scalar_prefetch=1,
-            grid=(1,),
+            grid=(count,),
             in_specs=in_specs,
-            out_specs=[tile_spec, pl.BlockSpec((1, 1, p_rows, LANES), new_probe_at)],
+            out_specs=[tile_spec, pl.BlockSpec(probe_shape, lambda i, w: (0, 0, 0, 0))],
         ),
-        out_shape=[
-            jax.ShapeDtypeStruct(tiles.shape, F32),
-            jax.ShapeDtypeStruct((half, 2, n // groups, n), F32),
-        ],
-        input_output_aliases=aliases,
-        compiler_params=BIG,
-        cost_estimate=pl.CostEstimate(
-            flops=2 * main * LANES, bytes_accessed=12 * main * LANES, transcendentals=0
-        ),
+        out_shape=[jax.ShapeDtypeStruct(tiles.shape, F32), jax.ShapeDtypeStruct(probe_shape, F32)],
+        compiler_params=BIG,
         name="update",
-    )(where, *operands)
+    )(where, tiles, probe, *chunks, *chunks)
 
 
 def local(objects, probe, measured, send_list, corner_slot, offsets):
@@ -488,12 +495,12 @@
                 if not (final and h == 0):
                     behind[h] = lax.ppermute(behind[h], "batch", backward)
                     found.append((z + step, h, behind[h]))
-        state = None
-        for place, h, chunk in found:
-            row = lax.rem(place + z_size, z_size) * 2 + h
-            where = jnp.stack([row, cut, member]).astype(jnp.int32)
-            state = update(where, tiles, chunk, probe, state, groups, p_rows, rate, half)
-    return (state[0][None], state[1])
+        places = [lax.rem(place + z_size, z_size) * 2 + h for place, h, _ in found]
+        where = jnp.stack(places + [cut, member]).astype(jnp.int32)
+        new_tiles, new_probe = update(
+            where, tiles, probe, [chunk for _, _, chunk in found], groups, p_rows, rate
+        )
+    return (new_tiles[None], new_probe)
 
 
 def solution(mesh):

time: 273 us -> 235 us (0.86)
  Pallas kernels: 93.8 us -> 48.4 us
  blocking collectives: 24.8 us -> 41.8 us
  other arithmetic: 10.4 us -> 0.96 us
    pallas_call x16 -> x1, Pallas kernels: 39.5 us -> 8.51 us  [update(): pl.pallas_call(partial(update_kernel, probe_rate, half, p_rows), grid_spe...]
    all_to_all x0 -> x1, blocking collectives: none -> 15 us  [local(): lax.all_to_all(summed, ('batch', 'tile'), split_axis=0, concat_axis=0, ax...]
    pallas_call x1, Pallas kernels: 35 us -> 20.6 us  [wave_terms(): pl.pallas_call(wave_kernel, in_specs=[pl.BlockSpec(memory_space=pltpu.SME...]
    another operation x15 -> x0, other arithmetic: 9.45 us -> none  [local(): where = jnp.stack([row, cut, member]).astype(jnp.int32)]
    all_to_all x1 -> x0, waiting for transfers between devices: 7.7 us -> none  [local(): lax.all_to_all(summed, ('batch', 'tile'), split_axis=0, concat_axis=0, ax...]
    all_to_all x1 -> x0, starting transfers between devices: 4.79 us -> none  [local(): lax.all_to_all(summed, ('batch', 'tile'), split_axis=0, concat_axis=0, ax...]
    ppermute x7, waiting for transfers between devices: 0.02 us -> 4.7 us  [local(): behind[h] = lax.ppermute(behind[h], 'batch', backward)]
    ppermute x7, starting transfers between devices: 17 us -> 20.8 us  [local(): behind[h] = lax.ppermute(behind[h], 'batch', backward)]
  transfers between devices with their start and end apart: 18 -> 17, of which waited for: 7 -> 12; matrix products, arithmetic and copies ran while one was open for 4% -> 1% of each run, Pallas kernels for 14% -> 0%
where the time goes in v2:
time: 235 us; the launch traced here: 234 us
  waiting for transfers between devices  94.3 us (40%)
  Pallas kernels  48.4 us (21%)
  starting transfers between devices  43.2 us (18%)
  blocking collectives  41.8 us (18%)
  local copies, waits for them, and re-layouts  3.98 us (2%)
    all_to_all x1, waiting for transfers between devices, local(): lax.all_to_all(outgoing, 'tile', split_axis=0, concat_axis=0, tiled=True)  54.8 us
    all_to_all x1, blocking collectives, local(): lax.all_to_all(pieces, 'tile', split_axis=0, concat_axis=0, tiled=True)  26.8 us
    ppermute x7, starting transfers between devices, local(): behind[h] = lax.ppermute(behind[h], 'batch', backward)  20.8 us
    pallas_call x1, Pallas kernels, wave_terms(): pl.pallas_call(wave_kernel, in_specs=[pl.BlockSpec(memory_space=pltpu.SME...  20.6 us
    all_to_all x1, waiting for transfers between devices, local(): lax.all_to_all(pieces, 'batch', split_axis=0, concat_axis=0, tiled=True)  19.8 us
    all_to_all x1, blocking collectives, local(): lax.all_to_all(summed, ('batch', 'tile'), split_axis=0, concat_axis=0, ax...  15 us
    ppermute x7, waiting for transfers between devices, local(): ahead[h] = lax.ppermute(ahead[h], 'batch', onward)  13.6 us
    all_to_all x1, starting transfers between devices, local(): lax.all_to_all(pieces, 'batch', split_axis=0, concat_axis=0, tiled=True)  13.5 us
  transfers between devices with their start and end apart: 17, of which 12 were waited for; matrix products, arithmetic and copies ran while one was open for 1% of the time, Pallas kernels for 0%

profile of v2, /device:TPU:2, one launch (start us, length us, event | category | flops | bytes accessed | tf_op | source)
XLA Modules:
  0.0 233.7 jit_solution(14800202073277344133)
XLA Ops:
  0.6 7.5 %gather_tiles.1 = f32[8,1024,128]{2,1,0:T(8,128)} custom-call(s32[8]{0:T(128)} %bitcast.29, f32[8,2,256,256]{3,2,1,0:T(8,128)} %bitcast.26), custom_call_target="tpu_custom_call" | custom-call | tf_op jit(solution)/shard_map/fetch_tiles/gather_tiles/pallas_call | solution.py:89
  8.2 6.7 %all-to-all-start = ((f32[8,1024,128]{2,1,0:T(8,128)}), f32[8,1024,128]{2,1,0:T(8,128)}, u32[]{:S(2)}, u32[]{:S(2)}) async-start(f32[8,1024,128]{2,1,0:T(8,128)} %gather_tiles.1), calls=%async_computation | async-start | bytes 8388608 | tf_op jit(solution)/shard_map/fetch_tiles/all_to_all | solution.py:451
  15.6 54.8 %all-to-all-done.c0_ref.c1_ref.c2_ref.c3_ref = f32[8,1024,128]{2,1,0:T(8,128)} async-done(((f32[8,1024,128]{2,1,0:T(8,128)}), f32[8,1024,128]{2,1,0:T(8,128)}, u32[]{:S(2)}, u32[]{:S(2)}) %all-to-all-start) | async-done | bytes 4194336 | tf_op jit(solution)/shard_map/fetch_tiles/all_to_all | solution.py:451
  70.4 3.1 %select_corners.1.own_ref = f32[1024,128]{1,0:T(8,128)} custom-call(s32[8]{0:T(128)} %pad_add_fusion.info_ref, f32[8,1024,128]{2,1,0:T(8,128)} %all-to-all-done.c0_ref.c1_ref.c2_ref.c3_ref, f32[8,1024,128]{2,1,0:T(8,128)} %all-to-all-done.c0_ref.c1_ref.c2_ref.c3_ref, f32[8,1024,128]{2,1,0:T(8,128)} %all-to-all-done.c0_ref.c1_ref.c2_ref.c3_ref, ...), custom_call_target="tpu_custom_call" | custom-call | tf_op jit(solution)/shard_map/fetch_tiles/select_corners/pallas_call | solution.py:119
  76.4 20.6 %wave_terms.1 = f32[8,392,128]{2,1,0:T(8,128)} custom-call(s32[8]{0:T(128)} %pad_add_fusion.info_ref, f32[1024,128]{1,0:T(8,128)} %select_corners.1.own_ref, f32[1024,128]{1,0:T(8,128)} %copy-done.14, f32[4,2,256,256]{3,2,1,0:T(8,128)} %probe_ref.3, f32[1,256,256]{2,1,0:T(8,128)} %data_ref.1, f32[8,128]{1,0:T(8,128)} %scatter.4.meta_ref, ...), custom_call_target="tpu_custom_call" | custom-call | tf_op jit(solution)/shard_map/waves/wave_terms/pallas_call | solution.py:235
  96.9 26.8 %all_to_all.20.in_ref = f32[8,392,128]{2,1,0:T(8,128)} all-to-all(f32[8,392,128]{2,1,0:T(8,128)} %wave_terms.1), channel_id=1, replica_groups=mesh['batch'=16,'tile'=8,'cuts'=2] {'tile'}, dimensions={0} | all-to-all | bytes 3211264 | tf_op jit(solution)/shard_map/return_terms/all_to_all | solution.py:457
  123.8 2.4 %regroup.1 = f32[16,88,128]{2,1,0:T(8,128)} custom-call(f32[8,392,128]{2,1,0:T(8,128)} %all_to_all.20.in_ref), custom_call_target="tpu_custom_call" | custom-call | tf_op jit(solution)/shard_map/return_terms/regroup/pallas_call | solution.py:275
  126.2 13.5 %all-to-all-start.2 = ((f32[16,88,128]{2,1,0:T(8,128)}), f32[16,88,128]{2,1,0:T(8,128)S(1)}, u32[]{:S(2)}, u32[]{:S(2)}) async-start(f32[16,88,128]{2,1,0:T(8,128)} %regroup.1), calls=%async_computation.2 | async-start | bytes 1441792 | tf_op jit(solution)/shard_map/return_terms/all_to_all | solution.py:459
  139.7 19.8 %all-to-all-done.2.in_ref = f32[16,88,128]{2,1,0:T(8,128)S(1)} async-done(((f32[16,88,128]{2,1,0:T(8,128)}), f32[16,88,128]{2,1,0:T(8,128)S(1)}, u32[]{:S(2)}, u32[]{:S(2)}) %all-to-all-start.2) | async-done | bytes 720928 | tf_op jit(solution)/shard_map/return_terms/all_to_all | solution.py:459
  161.0 4.3 %reduce_positions.1 = f32[16,80,128]{2,1,0:T(8,128)} custom-call(s32[8]{0:T(128)} %pad_add_fusion.info_ref, s32[1024]{0:T(1024)} %reshape.81.table_ref, f32[16,88,128]{2,1,0:T(8,128)} %copy-done), custom_call_target="tpu_custom_call" | custom-call | tf_op jit(solution)/shard_map/return_terms/reduce_positions/pallas_call | solution.py:329
  165.3 15.0 %all_to_all.21.in_ref = f32[16,80,128]{2,1,0:T(8,128)} all-to-all(f32[16,80,128]{2,1,0:T(8,128)} %reduce_positions.1), channel_id=1, replica_groups={{0,2,4,6,8,10,12,14,16,18,20,22,24,26,28,30},{32,34,36,38,40,42,44,46,4..., dimensions={0} | all-to-all | bytes 1310720 | tf_op jit(solution)/shard_map/return_terms/all_to_all | solution.py:475
  180.3 2.0 pack.1
  182.5 3.0 %collective-permute-start.4 = (f32[528,128]{1,0:T(8,128)}, f32[528,128]{1,0:T(8,128)S(1)}, u32[]{:S(2)}, u32[]{:S(2)}) collective-permute-start(f32[528,128]{1,0:T(8,128)} %get-tuple-element.19.refs_1_.refs_17_), channel_id=1, source_target_pairs={{0,224},{16,240},{32,0},{48,16},{64,32},{80,48},{96,64},{112,80},{... | collective-permute-start | bytes 811016 | tf_op jit(solution)/shard_map/spread_sums/ppermute | solution.py:496
  185.5 2.0 collective-permute-start.3
  187.5 4.9 %collective-permute-done.1.refs_2_.refs_18_ = f32[528,128]{1,0:T(8,128)S(1)} collective-permute-done((f32[528,128]{1,0:T(8,128)}, f32[528,128]{1,0:T(8,128)S(1)}, u32[]{:S(2)}, u32[]{:S(2)}) %collective-permute-start.1) | collective-permute-done | bytes 270368 | tf_op jit(solution)/shard_map/spread_sums/ppermute | solution.py:493
  192.7 3.6 %collective-permute-start.8 = (f32[528,128]{1,0:T(8,128)S(1)}, f32[528,128]{1,0:T(8,128)S(1)}, u32[]{:S(2)}, u32[]{:S(2)}) collective-permute-start(f32[528,128]{1,0:T(8,128)S(1)} %collective-permute-done.4.refs_5_.refs_21_), channel_id=1, source_target_pairs={{0,224},{16,240},{32,0},{48,16},{64,32},{80,48},{96,64},{112,80},{... | collective-permute-start | bytes 811016 | tf_op jit(solution)/shard_map/spread_sums/ppermute | solution.py:496
  196.3 2.2 collective-permute-done.2.refs_3_.refs_19_
  198.5 3.6 %collective-permute-start.6 = (f32[528,128]{1,0:T(8,128)S(1)}, f32[528,128]{1,0:T(8,128)S(1)}, u32[]{:S(2)}, u32[]{:S(2)}) collective-permute-start(f32[528,128]{1,0:T(8,128)S(1)} %collective-permute-done.2.refs_3_.refs_19_), channel_id=1, source_target_pairs={{0,224},{16,240},{32,0},{48,16},{64,32},{80,48},{96,64},{112,80},{... | collective-permute-start | bytes 811016 | tf_op jit(solution)/shard_map/spread_sums/ppermute | solution.py:496
  204.2 3.7 %collective-permute-start.12 = (f32[528,128]{1,0:T(8,128)S(1)}, f32[528,128]{1,0:T(8,128)S(1)}, u32[]{:S(2)}, u32[]{:S(2)}) collective-permute-start(f32[528,128]{1,0:T(8,128)S(1)} %collective-permute-done.8.refs_9_.refs_25_), channel_id=1, source_target_pairs={{0,224},{16,240},{32,0},{48,16},{64,32},{80,48},{96,64},{112,80},{... | collective-permute-start | bytes 811016 | tf_op jit(solution)/shard_map/spread_sums/ppermute | solution.py:496
  207.9 2.1 collective-permute-done.6.refs_7_.refs_23_
  210.0 3.7 %collective-permute-start.10 = (f32[528,128]{1,0:T(8,128)S(1)}, f32[528,128]{1,0:T(8,128)S(1)}, u32[]{:S(2)}, u32[]{:S(2)}) collective-permute-start(f32[528,128]{1,0:T(8,128)S(1)} %collective-permute-done.6.refs_7_.refs_23_), channel_id=1, source_target_pairs={{0,224},{16,240},{32,0},{48,16},{64,32},{80,48},{96,64},{112,80},{... | collective-permute-start | bytes 811016 | tf_op jit(solution)/shard_map/spread_sums/ppermute | solution.py:496
  215.6 3.2 %collective-permute-start.14 = (f32[528,128]{1,0:T(8,128)S(1)}, f32[528,128]{1,0:T(8,128)}, u32[]{:S(2)}, u32[]{:S(2)}) collective-permute-start(f32[528,128]{1,0:T(8,128)S(1)} %collective-permute-done.12.refs_13_.refs_29_), channel_id=1, source_target_pairs={{0,224},{16,240},{32,0},{48,16},{64,32},{80,48},{96,64},{112,80},{... | collective-permute-start | bytes 811016 | tf_op jit(solution)/shard_map/spread_sums/ppermute | solution.py:496
  221.4 2.9 %collective-permute-done.13.refs_14_.refs_30_ = f32[528,128]{1,0:T(8,128)S(1)} collective-permute-done((f32[528,128]{1,0:T(8,128)S(1)}, f32[528,128]{1,0:T(8,128)S(1)}, u32[]{:S(2)}, u32[]{:S(2)}) %collective-permute-start.13) | collective-permute-done | bytes 270368 | tf_op jit(solution)/shard_map/spread_sums/ppermute | solution.py:493
  225.0 8.5 %update.1 = (f32[8,2,256,256]{3,2,1,0:T(8,128)}, f32[2,2,32,256]{3,2,1,0:T(8,128)}) custom-call(s32[18]{0:T(128)} %stack.79.where_ref, f32[8,2,256,256]{3,2,1,0:T(8,128)} %bitcast.27, f32[4,2,256,256]{3,2,1,0:T(8,128)} %probe_ref.3, f32[528,128]{1,0:T(8,128)} %get-tuple-element.18.refs_0_.refs_16_, f32[528,128]{1,0:T(8,128)} %get-tuple-element.19.refs_1_.refs_17_, ...), custom_call_target="tpu_custom_call" | custom-call | tf_op jit(solution)/shard_map/spread_sums/update/pallas_call | solution.py:412
  (71 shorter events, 12.8 us)
Async XLA Ops:
  8.2 62.2 %all-to-all-start = ((f32[8,1024,128]{2,1,0:T(8,128)}), f32[8,1024,128]{2,1,0:T(8,128)}, u32[]{:S(2)}, u32[]{:S(2)}) async-start(f32[8,1024,128]{2,1,0:T(8,128)} %gather_tiles.1), calls=%async_computation | async-start | bytes 8388608 | tf_op jit(solution)/shard_map/fetch_tiles/all_to_all | solution.py:451
  15.6 57.9 %copy-start.15 = (s32[1,1,8]{2,1,0:T(1,128)S(1)}, s32[1,1,8]{2,1,0:T(1,128)}, u32[]{:S(2)}) copy-start(s32[1,1,8]{2,1,0:T(1,128)} %param.19) | copy-start | bytes 100
  73.4 2.1 collective-permute-start
  126.2 33.4 %all-to-all-start.2 = ((f32[16,88,128]{2,1,0:T(8,128)}), f32[16,88,128]{2,1,0:T(8,128)S(1)}, u32[]{:S(2)}, u32[]{:S(2)}) async-start(f32[16,88,128]{2,1,0:T(8,128)} %regroup.1), calls=%async_computation.2 | async-start | bytes 1441792 | tf_op jit(solution)/shard_map/return_terms/all_to_all | solution.py:459
  182.3 10.2 %collective-permute-start.1 = (f32[528,128]{1,0:T(8,128)}, f32[528,128]{1,0:T(8,128)S(1)}, u32[]{:S(2)}, u32[]{:S(2)}) collective-permute-start(f32[528,128]{1,0:T(8,128)} %get-tuple-element.18.refs_0_.refs_16_), channel_id=1, source_target_pairs={{0,32},{16,48},{32,64},{48,80},{64,96},{80,112},{96,128},{112,144}... | collective-permute-start | bytes 811016 | tf_op jit(solution)/shard_map/spread_sums/ppermute | solution.py:493
  182.5 10.2 %collective-permute-start.4 = (f32[528,128]{1,0:T(8,128)}, f32[528,128]{1,0:T(8,128)S(1)}, u32[]{:S(2)}, u32[]{:S(2)}) collective-permute-start(f32[528,128]{1,0:T(8,128)} %get-tuple-element.19.refs_1_.refs_17_), channel_id=1, source_target_pairs={{0,224},{16,240},{32,0},{48,16},{64,32},{80,48},{96,64},{112,80},{... | collective-permute-start | bytes 811016 | tf_op jit(solution)/shard_map/spread_sums/ppermute | solution.py:496
  185.5 13.0 %collective-permute-start.2 = (f32[528,128]{1,0:T(8,128)}, f32[528,128]{1,0:T(8,128)S(1)}, u32[]{:S(2)}, u32[]{:S(2)}) collective-permute-start(f32[528,128]{1,0:T(8,128)} %get-tuple-element.18.refs_0_.refs_16_), channel_id=1, source_target_pairs={{0,224},{16,240},{32,0},{48,16},{64,32},{80,48},{96,64},{112,80},{... | collective-permute-start | bytes 811016 | tf_op jit(solution)/shard_map/spread_sums/ppermute | solution.py:496
  185.5 16.6 %collective-permute-start.3 = (f32[528,128]{1,0:T(8,128)}, f32[528,128]{1,0:T(8,128)S(1)}, u32[]{:S(2)}, u32[]{:S(2)}) collective-permute-start(f32[528,128]{1,0:T(8,128)} %get-tuple-element.19.refs_1_.refs_17_), channel_id=1, source_target_pairs={{0,32},{16,48},{32,64},{48,80},{64,96},{80,112},{96,128},{112,144}... | collective-permute-start | bytes 811016 | tf_op jit(solution)/shard_map/spread_sums/ppermute | solution.py:493
  192.5 31.8 %copy-start.1 = (f32[528,128]{1,0:T(8,128)}, f32[528,128]{1,0:T(8,128)S(1)}, u32[]{:S(2)}) copy-start(f32[528,128]{1,0:T(8,128)S(1)} %collective-permute-done.1.refs_2_.refs_18_) | copy-start | bytes 811012
  192.5 11.6 %collective-permute-start.5 = (f32[528,128]{1,0:T(8,128)S(1)}, f32[528,128]{1,0:T(8,128)S(1)}, u32[]{:S(2)}, u32[]{:S(2)}) collective-permute-start(f32[528,128]{1,0:T(8,128)S(1)} %collective-permute-done.1.refs_2_.refs_18_), channel_id=1, source_target_pairs={{0,32},{16,48},{32,64},{48,80},{64,96},{80,112},{96,128},{112,144}... | collective-permute-start | bytes 811016 | tf_op jit(solution)/shard_map/spread_sums/ppermute | solution.py:493
  192.7 31.6 %copy-start.2 = (f32[528,128]{1,0:T(8,128)}, f32[528,128]{1,0:T(8,128)S(1)}, u32[]{:S(2)}) copy-start(f32[528,128]{1,0:T(8,128)S(1)} %collective-permute-done.4.refs_5_.refs_21_) | copy-start | bytes 811012
  192.7 11.5 %collective-permute-start.8 = (f32[528,128]{1,0:T(8,128)S(1)}, f32[528,128]{1,0:T(8,128)S(1)}, u32[]{:S(2)}, u32[]{:S(2)}) collective-permute-start(f32[528,128]{1,0:T(8,128)S(1)} %collective-permute-done.4.refs_5_.refs_21_), channel_id=1, source_target_pairs={{0,224},{16,240},{32,0},{48,16},{64,32},{80,48},{96,64},{112,80},{... | collective-permute-start | bytes 811016 | tf_op jit(solution)/shard_map/spread_sums/ppermute | solution.py:496
  198.5 25.8 %copy-start.3 = (f32[528,128]{1,0:T(8,128)}, f32[528,128]{1,0:T(8,128)S(1)}, u32[]{:S(2)}) copy-start(f32[528,128]{1,0:T(8,128)S(1)} %collective-permute-done.2.refs_3_.refs_19_) | copy-start | bytes 811012
  198.5 11.5 %collective-permute-start.6 = (f32[528,128]{1,0:T(8,128)S(1)}, f32[528,128]{1,0:T(8,128)S(1)}, u32[]{:S(2)}, u32[]{:S(2)}) collective-permute-start(f32[528,128]{1,0:T(8,128)S(1)} %collective-permute-done.2.refs_3_.refs_19_), channel_id=1, source_target_pairs={{0,224},{16,240},{32,0},{48,16},{64,32},{80,48},{96,64},{112,80},{... | collective-permute-start | bytes 811016 | tf_op jit(solution)/shard_map/spread_sums/ppermute | solution.py:496
  202.1 22.2 %copy-start.4 = (f32[528,128]{1,0:T(8,128)}, f32[528,128]{1,0:T(8,128)S(1)}, u32[]{:S(2)}) copy-start(f32[528,128]{1,0:T(8,128)S(1)} %collective-permute-done.3.refs_4_.refs_20_) | copy-start | bytes 811012
  202.1 11.6 %collective-permute-start.7 = (f32[528,128]{1,0:T(8,128)S(1)}, f32[528,128]{1,0:T(8,128)S(1)}, u32[]{:S(2)}, u32[]{:S(2)}) collective-permute-start(f32[528,128]{1,0:T(8,128)S(1)} %collective-permute-done.3.refs_4_.refs_20_), channel_id=1, source_target_pairs={{0,32},{16,48},{32,64},{48,80},{64,96},{80,112},{96,128},{112,144}... | collective-permute-start | bytes 811016 | tf_op jit(solution)/shard_map/spread_sums/ppermute | solution.py:493
  204.1 20.3 %copy-start.5 = (f32[528,128]{1,0:T(8,128)}, f32[528,128]{1,0:T(8,128)S(1)}, u32[]{:S(2)}) copy-start(f32[528,128]{1,0:T(8,128)S(1)} %collective-permute-done.5.refs_6_.refs_22_) | copy-start | bytes 811012
  204.1 11.5 %collective-permute-start.9 = (f32[528,128]{1,0:T(8,128)S(1)}, f32[528,128]{1,0:T(8,128)S(1)}, u32[]{:S(2)}, u32[]{:S(2)}) collective-permute-start(f32[528,128]{1,0:T(8,128)S(1)} %collective-permute-done.5.refs_6_.refs_22_), channel_id=1, source_target_pairs={{0,32},{16,48},{32,64},{48,80},{64,96},{80,112},{96,128},{112,144}... | collective-permute-start | bytes 811016 | tf_op jit(solution)/shard_map/spread_sums/ppermute | solution.py:493
  204.2 20.1 %copy-start.6 = (f32[528,128]{1,0:T(8,128)}, f32[528,128]{1,0:T(8,128)S(1)}, u32[]{:S(2)}) copy-start(f32[528,128]{1,0:T(8,128)S(1)} %collective-permute-done.8.refs_9_.refs_25_) | copy-start | bytes 811012
  204.2 11.4 %collective-permute-start.12 = (f32[528,128]{1,0:T(8,128)S(1)}, f32[528,128]{1,0:T(8,128)S(1)}, u32[]{:S(2)}, u32[]{:S(2)}) collective-permute-start(f32[528,128]{1,0:T(8,128)S(1)} %collective-permute-done.8.refs_9_.refs_25_), channel_id=1, source_target_pairs={{0,224},{16,240},{32,0},{48,16},{64,32},{80,48},{96,64},{112,80},{... | collective-permute-start | bytes 811016 | tf_op jit(solution)/shard_map/spread_sums/ppermute | solution.py:496
  210.0 9.5 %collective-permute-start.10 = (f32[528,128]{1,0:T(8,128)S(1)}, f32[528,128]{1,0:T(8,128)S(1)}, u32[]{:S(2)}, u32[]{:S(2)}) collective-permute-start(f32[528,128]{1,0:T(8,128)S(1)} %collective-permute-done.6.refs_7_.refs_23_), channel_id=1, source_target_pairs={{0,224},{16,240},{32,0},{48,16},{64,32},{80,48},{96,64},{112,80},{... | collective-permute-start | bytes 811016 | tf_op jit(solution)/shard_map/spread_sums/ppermute | solution.py:496
  213.7 7.7 %collective-permute-start.11 = (f32[528,128]{1,0:T(8,128)S(1)}, f32[528,128]{1,0:T(8,128)S(1)}, u32[]{:S(2)}, u32[]{:S(2)}) collective-permute-start(f32[528,128]{1,0:T(8,128)S(1)} %collective-permute-done.7.refs_8_.refs_24_), channel_id=1, source_target_pairs={{0,32},{16,48},{32,64},{48,80},{64,96},{80,112},{96,128},{112,144}... | collective-permute-start | bytes 811016 | tf_op jit(solution)/shard_map/spread_sums/ppermute | solution.py:493
  215.6 8.7 %collective-permute-start.13 = (f32[528,128]{1,0:T(8,128)S(1)}, f32[528,128]{1,0:T(8,128)S(1)}, u32[]{:S(2)}, u32[]{:S(2)}) collective-permute-start(f32[528,128]{1,0:T(8,128)S(1)} %collective-permute-done.9.refs_10_.refs_26_), channel_id=1, source_target_pairs={{0,32},{16,48},{32,64},{48,80},{64,96},{80,112},{96,128},{112,144}... | collective-permute-start | bytes 811016 | tf_op jit(solution)/shard_map/spread_sums/ppermute | solution.py:493
  215.6 8.7 %collective-permute-start.14 = (f32[528,128]{1,0:T(8,128)S(1)}, f32[528,128]{1,0:T(8,128)}, u32[]{:S(2)}, u32[]{:S(2)}) collective-permute-start(f32[528,128]{1,0:T(8,128)S(1)} %collective-permute-done.12.refs_13_.refs_29_), channel_id=1, source_target_pairs={{0,224},{16,240},{32,0},{48,16},{64,32},{80,48},{96,64},{112,80},{... | collective-permute-start | bytes 811016 | tf_op jit(solution)/shard_map/spread_sums/ppermute | solution.py:496
  (11 other events, 66.8 us)

commit v3 on v2

--- a/solution.py
+++ b/solution.py
@@ -13,7 +13,8 @@
 OBJECT_RATE = 0.02
 PROBE_RATE = 0.05
 LANES = 128
-BIG = pltpu.CompilerParams(vmem_limit_bytes=56 * 1024 * 1024)
+BIG = pltpu.CompilerParams(vmem_limit_bytes=32 * 1024 * 1024)
+SMALL = pltpu.CompilerParams(vmem_limit_bytes=14 * 1024 * 1024)
 F32 = jnp.float32
 BF16 = jnp.bfloat16
 
@@ -76,58 +77,111 @@
 
 def gather_kernel(pick_ref, tile_ref, out_ref):
     n = tile_ref.shape[-1]
-    for part in range(2):
-        for side in range(n // LANES):
-            panel = part * (n // LANES) + side
-            out_ref[0, panel * n : (panel + 1) * n, :] = tile_ref[0, part, :, side * LANES : (side + 1) * LANES]
-
-
-def gather_tiles(pick, tiles):
+    for side in range(n // LANES):
+        out_ref[0, side * n : (side + 1) * n, :] = tile_ref[0, 0, :, side * LANES : (side + 1) * LANES]
+
+
+def gather_parts(pick, tiles, part):
     count = pick.shape[0]
     n = tiles.shape[-1]
-    rows = 2 * n * (n // LANES)
+    rows = n * (n // LANES)
     return pl.pallas_call(
         gather_kernel,
         grid_spec=pltpu.PrefetchScalarGridSpec(
             num_scalar_prefetch=1,
             grid=(count,),
-            in_specs=[pl.BlockSpec((1, 2, n, n), lambda i, pick: (pick[i], 0, 0, 0))],
+            in_specs=[pl.BlockSpec((1, 1, n, n), lambda i, pick: (pick[i], part, 0, 0))],
             out_specs=pl.BlockSpec((1, rows, LANES), lambda i, pick: (i, 0, 0)),
         ),
         out_shape=jax.ShapeDtypeStruct((count, rows, LANES), F32),
-        compiler_params=BIG,
-        name="gather_tiles",
+        compiler_params=SMALL,
+        name="gather_parts",
     )(pick, tiles)
 
 
-def select_kernel(n, info_ref, c0_ref, c1_ref, c2_ref, c3_ref, out_ref):
-    y0, x0 = info_ref[4], info_ref[5]
+def select_kernel(note_ref, own_ref, re_ref, im_ref, out_ref):
+    n = own_ref.shape[-1]
     sides = n // LANES
-    for panel in range(2 * sides):
-        rows = slice(panel * n, (panel + 1) * n)
+    y0, x0, here, near = note_ref[4], note_ref[5], note_ref[6], note_ref[7]
+    for side in range(sides):
         u = lax.broadcasted_iota(jnp.int32, (n, LANES), 0)
-        v = lax.broadcasted_iota(jnp.int32, (n, LANES), 1) + (panel % sides) * LANES
+        v = lax.broadcasted_iota(jnp.int32, (n, LANES), 1) + side * LANES
         low, right = u < y0, v < x0
-        upper = jnp.where(right, c1_ref[0, rows, :], c0_ref[0, rows, :])
-        lower = jnp.where(right, c3_ref[0, rows, :], c2_ref[0, rows, :])
-        out_ref[rows, :] = jnp.where(low, lower, upper)
-
-
-def select_corners(info, arrived, n):
-    rows = arrived.shape[1]
-    spec = lambda k: pl.BlockSpec((1, rows, LANES), lambda i, info: (info[k], 0, 0))
-    return pl.pallas_call(
-        partial(select_kernel, n),
+        owner = jnp.where(
+            low,
+            jnp.where(right, note_ref[3], note_ref[2]),
+            jnp.where(right, note_ref[1], note_ref[0]),
+        )
+        lanes = slice(side * LANES, (side + 1) * LANES)
+        for part, far_ref in enumerate((re_ref, im_ref)):
+            far = far_ref[0, side * n : (side + 1) * n, :]
+            panel = part * sides + side
+            out_ref[panel * n : (panel + 1) * n, :] = jnp.where(
+                owner == here,
+                own_ref[0, part, :, lanes],
+                jnp.where(owner == near, far, 0.0),
+            )
+
+
+def select_cells(note, tiles, real, imag):
+    n = tiles.shape[-1]
+    rows = n * (n // LANES)
+    return pl.pallas_call(
+        select_kernel,
         grid_spec=pltpu.PrefetchScalarGridSpec(
             num_scalar_prefetch=1,
             grid=(1,),
-            in_specs=[spec(0), spec(1), spec(2), spec(3)],
-            out_specs=pl.BlockSpec((rows, LANES), lambda i, info: (0, 0)),
+            in_specs=[
+                pl.BlockSpec((1, 2, n, n), lambda i, note: (note[8], 0, 0, 0)),
+                pl.BlockSpec((1, rows, LANES), lambda i, note: (note[9], 0, 0)),
+                pl.BlockSpec((1, rows, LANES), lambda i, note: (note[9], 0, 0)),
+            ],
+            out_specs=pl.BlockSpec((2 * rows, LANES), lambda i, note: (0, 0)),
         ),
-        out_shape=jax.ShapeDtypeStruct((rows, LANES), F32),
-        compiler_params=BIG,
-        name="select_corners",
-    )(info, arrived, arrived, arrived, arrived)
+        out_shape=jax.ShapeDtypeStruct((2 * rows, LANES), F32),
+        compiler_params=SMALL,
+        name="select_cells",
+    )(note, tiles, real, imag)
+
+
+def fetch(tiles, send_row, note):
+    groups = lax.axis_size("tile")
+    batches = lax.axis_size("batch")
+    width = groups // 2
+    member = lax.axis_index("tile")
+    column, lower = lax.rem(member, width), lax.div(member, width)
+    near = lax.rem(member + width, groups)
+    lists = send_row.reshape(2, width)
+    far_row = lax.ppermute(send_row, "batch", [(i, i ^ 1) for i in range(batches)])
+    along = lambda d: [
+        (y * width + x, y * width + (x + d) % width) for y in range(2) for x in range(width)
+    ]
+    notes = {0: note}
+    for d in range(1, width):
+        notes[d] = lax.ppermute(note, "tile", along(-d))
+    across = lambda row: lax.dynamic_index_in_dim(row.reshape(2, width), 1 - lower, 0, keepdims=False)
+    same = [(t, (t + width) % groups) for t in range(groups)]
+    other = []
+    for b in range(batches):
+        for t in range(groups):
+            y = (b % 2) * 2 + t // width
+            step = (y + 1) % 4 if y % 2 == 1 else (y - 1) % 4
+            other.append(
+                (b * groups + t, (b // 2 * 2 + step // 2) * groups + step % 2 * width + t % width)
+            )
+    real = lax.ppermute(gather_parts(across(send_row), tiles, 0), "tile", same)
+    imag = lax.ppermute(gather_parts(across(far_row), tiles, 1), ("batch", "tile"), other)
+    mine = lax.dynamic_index_in_dim(lists, lower, 0, keepdims=False)
+    total = None
+    for d in (2, 1, 3, 0):
+        x = lax.rem(column + d, width)
+        pick = lax.dynamic_index_in_dim(mine, x, 0, keepdims=False)
+        extra = jnp.stack([member, near, pick, x]).astype(jnp.int32)
+        cells = select_cells(jnp.concatenate([notes[d], extra]), tiles, real, imag)
+        if d:
+            cells = lax.ppermute(cells, "tile", along(d))
+        total = cells if total is None else total + cells
+    return total
 
 
 def wave_kernel(
@@ -277,7 +331,7 @@
         in_specs=[whole],
         out_specs=whole,
         out_shape=jax.ShapeDtypeStruct((batches, groups * 8 + p_rows + 8, LANES), F32),
-        compiler_params=BIG,
+        compiler_params=SMALL,
         name="regroup",
     )(pieces)
 
@@ -332,7 +386,7 @@
         out_specs=whole,
         out_shape=jax.ShapeDtypeStruct((2 * groups, tiles * 8 // groups + p_rows, LANES), F32),
         scratch_shapes=[pltpu.VMEM((4, tiles * 8, LANES), F32)],
-        compiler_params=BIG,
+        compiler_params=SMALL,
         name="reduce_positions",
     )(info, table, pieces)
 
@@ -357,7 +411,7 @@
         in_specs=[pl.BlockSpec(memory_space=pltpu.SMEM), whole],
         out_specs=[whole, whole],
         out_shape=[jax.ShapeDtypeStruct((rows, LANES), F32)] * 2,
-        compiler_params=BIG,
+        compiler_params=SMALL,
         name="pack",
     )(place, pieces)
 
@@ -418,7 +472,7 @@
             out_specs=[tile_spec, pl.BlockSpec(probe_shape, lambda i, w: (0, 0, 0, 0))],
         ),
         out_shape=[jax.ShapeDtypeStruct(tiles.shape, F32), jax.ShapeDtypeStruct(probe_shape, F32)],
-        compiler_params=BIG,
+        compiler_params=SMALL,
         name="update",
     )(where, tiles, probe, *chunks, *chunks)
 
@@ -447,9 +501,8 @@
     meta = jnp.zeros((8, LANES), F32).at[0, : meta_row.shape[0]].set(meta_row)
 
     with jax.named_scope("fetch_tiles"):
-        outgoing = gather_tiles(send_list.reshape(-1), tiles)
-        arrived = lax.all_to_all(outgoing, "tile", split_axis=0, concat_axis=0, tiled=True)
-        own = select_corners(info, arrived, n)
+        note = jnp.concatenate([corner_slot.reshape(-1), offsets.reshape(-1)])
+        own = fetch(tiles, send_list.reshape(-1), note)
         other = lax.ppermute(own, "cuts", [(0, 1), (1, 0)])
     with jax.named_scope("waves"):
         pieces = wave_terms(info, own, other, probe, measured, meta, groups)

time: 235 us -> 224 us (0.953)
  local copies, waits for them, and re-layouts: 3.98 us -> 28 us
  waiting for transfers between devices: 94.3 us -> 71.7 us
  Pallas kernels: 48.4 us -> 35 us
  blocking collectives: 41.8 us -> 37.3 us
  starting transfers between devices: 43.2 us -> 46 us
    all_to_all x1 -> x0, waiting for transfers between devices: 54.8 us -> none  [local(): lax.all_to_all(outgoing, 'tile', split_axis=0, concat_axis=0, tiled=True)]
    ppermute x0 -> x9, waiting for transfers between devices: none -> 33 us  [the longest x3 14.6 us: fetch(): cells = lax.ppermute(cells, 'tile', along(d))]
    unnamed x36 -> x49, local copies, waits for them, and re-layouts: 1.46 us -> 23.7 us
    ppermute x0 -> x9, starting transfers between devices: none -> 12.9 us  [the longest x3 4.24 us: fetch(): cells = lax.ppermute(cells, 'tile', along(d))]
    all_to_all x1 -> x0, starting transfers between devices: 6.71 us -> none  [local(): lax.all_to_all(outgoing, 'tile', split_axis=0, concat_axis=0, tiled=True)]
    pallas_call x2 -> x6, Pallas kernels: 10.6 us -> 6.91 us  [the longest x4 4.14 us: select_cells(): pl.pallas_call(select_kernel, grid_spec=pltpu.PrefetchScalarGridSpec(num_...]
    all_to_all x1, starting transfers between devices: 13.5 us -> 9.88 us  [local(): lax.all_to_all(pieces, 'batch', split_axis=0, concat_axis=0, tiled=True)]
    pallas_call x1, Pallas kernels: 20.6 us -> 17.4 us  [wave_terms(): pl.pallas_call(wave_kernel, in_specs=[pl.BlockSpec(memory_space=pltpu.SME...]
  transfers between devices with their start and end apart: 17 -> 25, of which waited for: 12 -> 14; matrix products, arithmetic and copies ran while one was open for 1% -> 3% of each run, Pallas kernels for 0% -> 3%
where the time goes in v3:
time: 224 us; the launch traced here: 222 us
  waiting for transfers between devices  71.7 us (32%)
  starting transfers between devices  46 us (21%)
  blocking collectives  37.3 us (17%)
  Pallas kernels  35 us (16%)
  local copies, waits for them, and re-layouts  28 us (12%)
  other arithmetic  3.27 us (1%)
    all_to_all x1, blocking collectives, local(): lax.all_to_all(pieces, 'tile', split_axis=0, concat_axis=0, tiled=True)  24 us
    unnamed x49, local copies, waits for them, and re-layouts  23.7 us
    ppermute x7, starting transfers between devices, local(): behind[h] = lax.ppermute(behind[h], 'batch', backward)  20.6 us
    all_to_all x1, waiting for transfers between devices, local(): lax.all_to_all(pieces, 'batch', split_axis=0, concat_axis=0, tiled=True)  19.8 us
    pallas_call x1, Pallas kernels, wave_terms(): pl.pallas_call(wave_kernel, in_specs=[pl.BlockSpec(memory_space=pltpu.SME...  17.4 us
    ppermute x3, waiting for transfers between devices, fetch(): cells = lax.ppermute(cells, 'tile', along(d))  14.6 us
    ppermute x7, waiting for transfers between devices, local(): ahead[h] = lax.ppermute(ahead[h], 'batch', onward)  13.8 us
    all_to_all x1, blocking collectives, local(): lax.all_to_all(summed, ('batch', 'tile'), split_axis=0, concat_axis=0, ax...  13.3 us
  transfers between devices with their start and end apart: 25, of which 14 were waited for; matrix products, arithmetic and copies ran while one was open for 3% of the time, Pallas kernels for 3%

profile of v3, /device:TPU:2, one launch (start us, length us, event | category | flops | bytes accessed | tf_op | source)
XLA Modules:
  0.0 222.3 jit_solution(5023532291584409037)
XLA Ops:
  0.6 3.3 %collective-permute-start.2 = (s32[8]{0:T(128)}, s32[8]{0:T(128)S(1)}, u32[]{:S(2)}, u32[]{:S(2)}) collective-permute-start(s32[8]{0:T(128)} %bitcast.53), channel_id=1, source_target_pairs={{0,16},{16,0},{32,48},{48,32},{64,80},{80,64},{96,112},{112,96},{1... | collective-permute-start | bytes 104 | tf_op jit(solution)/shard_map/fetch_tiles/ppermute | solution.py:155
  22.3 11.1 %collective-permute-done.1.re_ref = f32[4,512,128]{2,1,0:T(8,128)S(1)} collective-permute-done((f32[4,512,128]{2,1,0:T(8,128)S(1)}, f32[4,512,128]{2,1,0:T(8,128)S(1)}, u32[]{:S(2)}, u32[]{:S(2)}) %collective-permute-start.1) | collective-permute-done | bytes 1048608 | tf_op jit(solution)/shard_map/fetch_tiles/ppermute | solution.py:172
  33.4 6.2 %collective-permute-done.3.im_ref = f32[4,512,128]{2,1,0:T(8,128)S(1)} collective-permute-done((f32[4,512,128]{2,1,0:T(8,128)}, f32[4,512,128]{2,1,0:T(8,128)S(1)}, u32[]{:S(2)}, u32[]{:S(2)}) %collective-permute-start.3) | collective-permute-done | bytes 1048608 | tf_op jit(solution)/shard_map/fetch_tiles/ppermute | solution.py:173
  42.4 2.2 collective-permute-start.4
  50.2 2.2 copy-done.3
  53.1 6.0 %collective-permute-done.4 = f32[1024,128]{1,0:T(8,128)} collective-permute-done((f32[1024,128]{1,0:T(8,128)S(1)}, f32[1024,128]{1,0:T(8,128)}, u32[]{:S(2)}, u32[]{:S(2)}) %collective-permute-start.4) | collective-permute-done | bytes 524320 | tf_op jit(solution)/shard_map/fetch_tiles/ppermute | solution.py:182
  59.1 8.6 %collective-permute-done.6 = f32[1024,128]{1,0:T(8,128)} collective-permute-done((f32[1024,128]{1,0:T(8,128)}, f32[1024,128]{1,0:T(8,128)}, u32[]{:S(2)}, u32[]{:S(2)}) %collective-permute-start.6) | collective-permute-done | bytes 524320 | tf_op jit(solution)/shard_map/fetch_tiles/ppermute | solution.py:182
  78.8 17.4 %wave_terms.1 = f32[8,392,128]{2,1,0:T(8,128)S(1)} custom-call(s32[8]{0:T(128)S(1)} %pad_add_fusion.info_ref, f32[1024,128]{1,0:T(8,128)S(1)} %add_add_fusion.own_ref, f32[1024,128]{1,0:T(8,128)} %collective-permute-done.9.other_ref, f32[4,2,256,256]{3,2,1,0:T(8,128)S(1)} %copy-done.5, f32[1,256,256]{2,1,0:T(8,128)S(1)} %copy-done.20, ...), custom_call_target="tpu_custom_call" | custom-call | tf_op jit(solution)/shard_map/waves/wave_terms/pallas_call | solution.py:289
  96.2 24.0 %all_to_all.15.in_ref = f32[8,392,128]{2,1,0:T(8,128)S(1)} all-to-all(f32[8,392,128]{2,1,0:T(8,128)S(1)} %wave_terms.1), channel_id=1, replica_groups=mesh['batch'=16,'tile'=8,'cuts'=2] {'tile'}, dimensions={0} | all-to-all | bytes 3211264 | tf_op jit(solution)/shard_map/return_terms/all_to_all | solution.py:510
  121.1 9.9 %all-to-all-start.1 = ((f32[16,88,128]{2,1,0:T(8,128)}), f32[16,88,128]{2,1,0:T(8,128)S(1)}, u32[]{:S(2)}, u32[]{:S(2)}) async-start(f32[16,88,128]{2,1,0:T(8,128)} %regroup.1), calls=%async_computation.1 | async-start | bytes 1441792 | tf_op jit(solution)/shard_map/return_terms/all_to_all | solution.py:512
  131.1 19.8 %all-to-all-done.1.in_ref = f32[16,88,128]{2,1,0:T(8,128)S(1)} async-done(((f32[16,88,128]{2,1,0:T(8,128)}), f32[16,88,128]{2,1,0:T(8,128)S(1)}, u32[]{:S(2)}, u32[]{:S(2)}) %all-to-all-start.1) | async-done | bytes 720928 | tf_op jit(solution)/shard_map/return_terms/all_to_all | solution.py:512
  151.8 2.5 %reduce_positions.1 = f32[16,80,128]{2,1,0:T(8,128)S(1)} custom-call(s32[8]{0:T(128)S(1)} %pad_add_fusion.info_ref, s32[1024]{0:T(1024)S(1)} %reshape.96.table_ref, f32[16,88,128]{2,1,0:T(8,128)S(1)} %all-to-all-done.1.in_ref), custom_call_target="tpu_custom_call" | custom-call | tf_op jit(solution)/shard_map/return_terms/reduce_positions/pallas_call | solution.py:383
  154.3 13.3 %all_to_all.16.in_ref = f32[16,80,128]{2,1,0:T(8,128)S(1)} all-to-all(f32[16,80,128]{2,1,0:T(8,128)S(1)} %reduce_positions.1), channel_id=1, replica_groups={{0,2,4,6,8,10,12,14,16,18,20,22,24,26,28,30},{32,34,36,38,40,42,44,46,4..., dimensions={0} | all-to-all | bytes 1310720 | tf_op jit(solution)/shard_map/return_terms/all_to_all | solution.py:528
  168.1 2.9 %collective-permute-start.13 = (f32[528,128]{1,0:T(8,128)S(1)}, f32[528,128]{1,0:T(8,128)S(1)}, u32[]{:S(2)}, u32[]{:S(2)}) collective-permute-start(f32[528,128]{1,0:T(8,128)S(1)} %get-tuple-element.19.refs_1_.refs_17_), channel_id=1, source_target_pairs={{0,224},{16,240},{32,0},{48,16},{64,32},{80,48},{96,64},{112,80},{... | collective-permute-start | bytes 811016 | tf_op jit(solution)/shard_map/spread_sums/ppermute | solution.py:549
  173.0 4.9 %collective-permute-done.10.refs_2_.refs_18_ = f32[528,128]{1,0:T(8,128)S(1)} collective-permute-done((f32[528,128]{1,0:T(8,128)S(1)}, f32[528,128]{1,0:T(8,128)S(1)}, u32[]{:S(2)}, u32[]{:S(2)}) %collective-permute-start.10) | collective-permute-done | bytes 270368 | tf_op jit(solution)/shard_map/spread_sums/ppermute | solution.py:546
  177.9 3.7 %collective-permute-start.17 = (f32[528,128]{1,0:T(8,128)S(1)}, f32[528,128]{1,0:T(8,128)S(1)}, u32[]{:S(2)}, u32[]{:S(2)}) collective-permute-start(f32[528,128]{1,0:T(8,128)S(1)} %collective-permute-done.13.refs_5_.refs_21_), channel_id=1, source_target_pairs={{0,224},{16,240},{32,0},{48,16},{64,32},{80,48},{96,64},{112,80},{... | collective-permute-start | bytes 811016 | tf_op jit(solution)/shard_map/spread_sums/ppermute | solution.py:549
  183.7 3.7 %collective-permute-start.15 = (f32[528,128]{1,0:T(8,128)S(1)}, f32[528,128]{1,0:T(8,128)}, u32[]{:S(2)}, u32[]{:S(2)}) collective-permute-start(f32[528,128]{1,0:T(8,128)S(1)} %collective-permute-done.11.refs_3_.refs_19_), channel_id=1, source_target_pairs={{0,224},{16,240},{32,0},{48,16},{64,32},{80,48},{96,64},{112,80},{... | collective-permute-start | bytes 811016 | tf_op jit(solution)/shard_map/spread_sums/ppermute | solution.py:549
  190.2 3.2 %collective-permute-start.21 = (f32[528,128]{1,0:T(8,128)S(1)}, f32[528,128]{1,0:T(8,128)}, u32[]{:S(2)}, u32[]{:S(2)}) collective-permute-start(f32[528,128]{1,0:T(8,128)S(1)} %collective-permute-done.17.refs_9_.refs_25_), channel_id=1, source_target_pairs={{0,224},{16,240},{32,0},{48,16},{64,32},{80,48},{96,64},{112,80},{... | collective-permute-start | bytes 811016 | tf_op jit(solution)/shard_map/spread_sums/ppermute | solution.py:549
  195.3 3.8 %collective-permute-start.19 = (f32[528,128]{1,0:T(8,128)}, f32[528,128]{1,0:T(8,128)}, u32[]{:S(2)}, u32[]{:S(2)}) collective-permute-start(f32[528,128]{1,0:T(8,128)} %collective-permute-done.15.refs_7_.refs_23_), channel_id=1, source_target_pairs={{0,224},{16,240},{32,0},{48,16},{64,32},{80,48},{96,64},{112,80},{... | collective-permute-start | bytes 811016 | tf_op jit(solution)/shard_map/spread_sums/ppermute | solution.py:549
  201.0 3.2 %collective-permute-start.23 = (f32[528,128]{1,0:T(8,128)}, f32[528,128]{1,0:T(8,128)}, u32[]{:S(2)}, u32[]{:S(2)}) collective-permute-start(f32[528,128]{1,0:T(8,128)} %collective-permute-done.21.refs_13_.refs_29_), channel_id=1, source_target_pairs={{0,224},{16,240},{32,0},{48,16},{64,32},{80,48},{96,64},{112,80},{... | collective-permute-start | bytes 811016 | tf_op jit(solution)/shard_map/spread_sums/ppermute | solution.py:549
  204.3 2.8 %collective-permute-done.20.refs_12_.refs_28_ = f32[528,128]{1,0:T(8,128)} collective-permute-done((f32[528,128]{1,0:T(8,128)}, f32[528,128]{1,0:T(8,128)}, u32[]{:S(2)}, u32[]{:S(2)}) %collective-permute-start.20) | collective-permute-done | bytes 270368 | tf_op jit(solution)/shard_map/spread_sums/ppermute | solution.py:546
  207.1 2.9 %collective-permute-done.22.refs_14_.refs_30_ = f32[528,128]{1,0:T(8,128)} collective-permute-done((f32[528,128]{1,0:T(8,128)}, f32[528,128]{1,0:T(8,128)}, u32[]{:S(2)}, u32[]{:S(2)}) %collective-permute-start.22) | collective-permute-done | bytes 270368 | tf_op jit(solution)/shard_map/spread_sums/ppermute | solution.py:546
  210.0 2.2 copy-done.4
  215.0 7.1 %update.1 = (f32[8,2,256,256]{3,2,1,0:T(8,128)}, f32[2,2,32,256]{3,2,1,0:T(8,128)}) custom-call(s32[18]{0:T(128)S(1)} %stack.105.where_ref, f32[8,2,256,256]{3,2,1,0:T(8,128)S(1)} %bitcast.45, f32[4,2,256,256]{3,2,1,0:T(8,128)S(1)} %copy-done.5, f32[528,128]{1,0:T(8,128)S(1)} %get-tuple-element.18.refs_0_.refs_16_, ...), custom_call_target="tpu_custom_call" | custom-call | tf_op jit(solution)/shard_map/spread_sums/update/pallas_call | solution.py:466
  (116 shorter events, 54.4 us)
Async XLA Ops:
  0.6 8.9 %collective-permute-start.2 = (s32[8]{0:T(128)}, s32[8]{0:T(128)S(1)}, u32[]{:S(2)}, u32[]{:S(2)}) collective-permute-start(s32[8]{0:T(128)} %bitcast.53), channel_id=1, source_target_pairs={{0,16},{16,0},{32,48},{48,32},{64,80},{80,64},{96,112},{112,96},{1... | collective-permute-start | bytes 104 | tf_op jit(solution)/shard_map/fetch_tiles/ppermute | solution.py:155
  8.7 24.7 %collective-permute-start.1 = (f32[4,512,128]{2,1,0:T(8,128)S(1)}, f32[4,512,128]{2,1,0:T(8,128)S(1)}, u32[]{:S(2)}, u32[]{:S(2)}) collective-permute-start(f32[4,512,128]{2,1,0:T(8,128)S(1)} %gather_parts.2), channel_id=1, source_target_pairs={{0,8},{2,10},{4,12},{6,14},{8,0},{10,2},{12,4},{14,6},{1,9},{3,11}... | collective-permute-start | bytes 3145736 | tf_op jit(solution)/shard_map/fetch_tiles/ppermute | solution.py:172
  13.9 25.8 %collective-permute-start.3 = (f32[4,512,128]{2,1,0:T(8,128)}, f32[4,512,128]{2,1,0:T(8,128)S(1)}, u32[]{:S(2)}, u32[]{:S(2)}) collective-permute-start(f32[4,512,128]{2,1,0:T(8,128)} %gather_parts.3), channel_id=1, source_target_pairs={{0,24},{2,26},{4,28},{6,30},{8,16},{10,18},{12,20},{14,22},{16,8},... | collective-permute-start | bytes 3145736 | tf_op jit(solution)/shard_map/fetch_tiles/ppermute | solution.py:173
  14.3 4.8 %collective-permute-start.7 = (s32[6]{0:T(128)S(1)}, s32[6]{0:T(128)S(1)}, u32[]{:S(2)}, u32[]{:S(2)}) collective-permute-start(s32[6]{0:T(128)S(1)} %pad_add_fusion.1), channel_id=1, source_target_pairs={{0,2},{2,4},{4,6},{6,0},{8,10},{10,12},{12,14},{14,8},{1,3},{3,5},... | collective-permute-start | bytes 80 | tf_op jit(solution)/shard_map/fetch_tiles/ppermute | solution.py:161
  15.8 4.0 %collective-permute-start.5 = (s32[6]{0:T(128)S(1)}, s32[6]{0:T(128)S(1)}, u32[]{:S(2)}, u32[]{:S(2)}) collective-permute-start(s32[6]{0:T(128)S(1)} %pad_add_fusion.1), channel_id=1, source_target_pairs={{0,6},{2,0},{4,2},{6,4},{8,14},{10,8},{12,10},{14,12},{1,7},{3,1},... | collective-permute-start | bytes 80 | tf_op jit(solution)/shard_map/fetch_tiles/ppermute | solution.py:161
  16.5 5.0 %collective-permute-start = (s32[6]{0:T(128)S(1)}, s32[6]{0:T(128)S(1)}, u32[]{:S(2)}, u32[]{:S(2)}) collective-permute-start(s32[6]{0:T(128)S(1)} %pad_add_fusion.1), channel_id=1, source_target_pairs={{0,4},{2,6},{4,0},{6,2},{8,12},{10,14},{12,8},{14,10},{1,5},{3,7},... | collective-permute-start | bytes 80 | tf_op jit(solution)/shard_map/fetch_tiles/ppermute | solution.py:161
  42.4 16.6 %collective-permute-start.4 = (f32[1024,128]{1,0:T(8,128)S(1)}, f32[1024,128]{1,0:T(8,128)}, u32[]{:S(2)}, u32[]{:S(2)}) collective-permute-start(f32[1024,128]{1,0:T(8,128)S(1)} %select_cells.4), channel_id=1, source_target_pairs={{0,4},{2,6},{4,0},{6,2},{8,12},{10,14},{12,8},{14,10},{1,5},{3,7},... | collective-permute-start | bytes 1572872 | tf_op jit(solution)/shard_map/fetch_tiles/ppermute | solution.py:182
  46.1 21.5 %collective-permute-start.6 = (f32[1024,128]{1,0:T(8,128)}, f32[1024,128]{1,0:T(8,128)}, u32[]{:S(2)}, u32[]{:S(2)}) collective-permute-start(f32[1024,128]{1,0:T(8,128)} %select_cells.5), channel_id=1, source_target_pairs={{0,2},{2,4},{4,6},{6,0},{8,10},{10,12},{12,14},{14,8},{1,3},{3,5},... | collective-permute-start | bytes 1572872 | tf_op jit(solution)/shard_map/fetch_tiles/ppermute | solution.py:182
  47.5 20.1 %collective-permute-start.8 = (f32[1024,128]{1,0:T(8,128)}, f32[1024,128]{1,0:T(8,128)}, u32[]{:S(2)}, u32[]{:S(2)}) collective-permute-start(f32[1024,128]{1,0:T(8,128)} %select_cells.6), channel_id=1, source_target_pairs={{0,6},{2,0},{4,2},{6,4},{8,14},{10,8},{12,10},{14,12},{1,7},{3,1},... | collective-permute-start | bytes 1572872 | tf_op jit(solution)/shard_map/fetch_tiles/ppermute | solution.py:182
  121.1 29.8 %all-to-all-start.1 = ((f32[16,88,128]{2,1,0:T(8,128)}), f32[16,88,128]{2,1,0:T(8,128)S(1)}, u32[]{:S(2)}, u32[]{:S(2)}) async-start(f32[16,88,128]{2,1,0:T(8,128)} %regroup.1), calls=%async_computation.1 | async-start | bytes 1441792 | tf_op jit(solution)/shard_map/return_terms/all_to_all | solution.py:512
  167.7 10.2 %collective-permute-start.10 = (f32[528,128]{1,0:T(8,128)S(1)}, f32[528,128]{1,0:T(8,128)S(1)}, u32[]{:S(2)}, u32[]{:S(2)}) collective-permute-start(f32[528,128]{1,0:T(8,128)S(1)} %get-tuple-element.18.refs_0_.refs_16_), channel_id=1, source_target_pairs={{0,32},{16,48},{32,64},{48,80},{64,96},{80,112},{96,128},{112,144}... | collective-permute-start | bytes 811016 | tf_op jit(solution)/shard_map/spread_sums/ppermute | solution.py:546
  168.1 9.8 %collective-permute-start.13 = (f32[528,128]{1,0:T(8,128)S(1)}, f32[528,128]{1,0:T(8,128)S(1)}, u32[]{:S(2)}, u32[]{:S(2)}) collective-permute-start(f32[528,128]{1,0:T(8,128)S(1)} %get-tuple-element.19.refs_1_.refs_17_), channel_id=1, source_target_pairs={{0,224},{16,240},{32,0},{48,16},{64,32},{80,48},{96,64},{112,80},{... | collective-permute-start | bytes 811016 | tf_op jit(solution)/shard_map/spread_sums/ppermute | solution.py:549
  171.0 12.7 %collective-permute-start.11 = (f32[528,128]{1,0:T(8,128)S(1)}, f32[528,128]{1,0:T(8,128)S(1)}, u32[]{:S(2)}, u32[]{:S(2)}) collective-permute-start(f32[528,128]{1,0:T(8,128)S(1)} %get-tuple-element.18.refs_0_.refs_16_), channel_id=1, source_target_pairs={{0,224},{16,240},{32,0},{48,16},{64,32},{80,48},{96,64},{112,80},{... | collective-permute-start | bytes 811016 | tf_op jit(solution)/shard_map/spread_sums/ppermute | solution.py:549
  171.0 16.4 %collective-permute-start.12 = (f32[528,128]{1,0:T(8,128)S(1)}, f32[528,128]{1,0:T(8,128)S(1)}, u32[]{:S(2)}, u32[]{:S(2)}) collective-permute-start(f32[528,128]{1,0:T(8,128)S(1)} %get-tuple-element.19.refs_1_.refs_17_), channel_id=1, source_target_pairs={{0,32},{16,48},{32,64},{48,80},{64,96},{80,112},{96,128},{112,144}... | collective-permute-start | bytes 811016 | tf_op jit(solution)/shard_map/spread_sums/ppermute | solution.py:546
  177.9 11.6 %collective-permute-start.14 = (f32[528,128]{1,0:T(8,128)S(1)}, f32[528,128]{1,0:T(8,128)S(1)}, u32[]{:S(2)}, u32[]{:S(2)}) collective-permute-start(f32[528,128]{1,0:T(8,128)S(1)} %collective-permute-done.10.refs_2_.refs_18_), channel_id=1, source_target_pairs={{0,32},{16,48},{32,64},{48,80},{64,96},{80,112},{96,128},{112,144}... | collective-permute-start | bytes 811016 | tf_op jit(solution)/shard_map/spread_sums/ppermute | solution.py:546
  177.9 12.3 %collective-permute-start.17 = (f32[528,128]{1,0:T(8,128)S(1)}, f32[528,128]{1,0:T(8,128)S(1)}, u32[]{:S(2)}, u32[]{:S(2)}) collective-permute-start(f32[528,128]{1,0:T(8,128)S(1)} %collective-permute-done.13.refs_5_.refs_21_), channel_id=1, source_target_pairs={{0,224},{16,240},{32,0},{48,16},{64,32},{80,48},{96,64},{112,80},{... | collective-permute-start | bytes 811016 | tf_op jit(solution)/shard_map/spread_sums/ppermute | solution.py:549
  183.7 11.6 %collective-permute-start.15 = (f32[528,128]{1,0:T(8,128)S(1)}, f32[528,128]{1,0:T(8,128)}, u32[]{:S(2)}, u32[]{:S(2)}) collective-permute-start(f32[528,128]{1,0:T(8,128)S(1)} %collective-permute-done.11.refs_3_.refs_19_), channel_id=1, source_target_pairs={{0,224},{16,240},{32,0},{48,16},{64,32},{80,48},{96,64},{112,80},{... | collective-permute-start | bytes 811016 | tf_op jit(solution)/shard_map/spread_sums/ppermute | solution.py:549
  187.4 11.7 %collective-permute-start.16 = (f32[528,128]{1,0:T(8,128)S(1)}, f32[528,128]{1,0:T(8,128)}, u32[]{:S(2)}, u32[]{:S(2)}) collective-permute-start(f32[528,128]{1,0:T(8,128)S(1)} %collective-permute-done.12.refs_4_.refs_20_), channel_id=1, source_target_pairs={{0,32},{16,48},{32,64},{48,80},{64,96},{80,112},{96,128},{112,144}... | collective-permute-start | bytes 811016 | tf_op jit(solution)/shard_map/spread_sums/ppermute | solution.py:546
  189.5 11.4 %collective-permute-start.18 = (f32[528,128]{1,0:T(8,128)S(1)}, f32[528,128]{1,0:T(8,128)}, u32[]{:S(2)}, u32[]{:S(2)}) collective-permute-start(f32[528,128]{1,0:T(8,128)S(1)} %collective-permute-done.14.refs_6_.refs_22_), channel_id=1, source_target_pairs={{0,32},{16,48},{32,64},{48,80},{64,96},{80,112},{96,128},{112,144}... | collective-permute-start | bytes 811016 | tf_op jit(solution)/shard_map/spread_sums/ppermute | solution.py:546
  190.2 10.7 %collective-permute-start.21 = (f32[528,128]{1,0:T(8,128)S(1)}, f32[528,128]{1,0:T(8,128)}, u32[]{:S(2)}, u32[]{:S(2)}) collective-permute-start(f32[528,128]{1,0:T(8,128)S(1)} %collective-permute-done.17.refs_9_.refs_25_), channel_id=1, source_target_pairs={{0,224},{16,240},{32,0},{48,16},{64,32},{80,48},{96,64},{112,80},{... | collective-permute-start | bytes 811016 | tf_op jit(solution)/shard_map/spread_sums/ppermute | solution.py:549
  195.3 9.0 %collective-permute-start.19 = (f32[528,128]{1,0:T(8,128)}, f32[528,128]{1,0:T(8,128)}, u32[]{:S(2)}, u32[]{:S(2)}) collective-permute-start(f32[528,128]{1,0:T(8,128)} %collective-permute-done.15.refs_7_.refs_23_), channel_id=1, source_target_pairs={{0,224},{16,240},{32,0},{48,16},{64,32},{80,48},{96,64},{112,80},{... | collective-permute-start | bytes 811016 | tf_op jit(solution)/shard_map/spread_sums/ppermute | solution.py:549
  199.1 8.0 %collective-permute-start.20 = (f32[528,128]{1,0:T(8,128)}, f32[528,128]{1,0:T(8,128)}, u32[]{:S(2)}, u32[]{:S(2)}) collective-permute-start(f32[528,128]{1,0:T(8,128)} %collective-permute-done.16.refs_8_.refs_24_), channel_id=1, source_target_pairs={{0,32},{16,48},{32,64},{48,80},{64,96},{80,112},{96,128},{112,144}... | collective-permute-start | bytes 811016 | tf_op jit(solution)/shard_map/spread_sums/ppermute | solution.py:546
  201.0 9.0 %collective-permute-start.22 = (f32[528,128]{1,0:T(8,128)}, f32[528,128]{1,0:T(8,128)}, u32[]{:S(2)}, u32[]{:S(2)}) collective-permute-start(f32[528,128]{1,0:T(8,128)} %collective-permute-done.18.refs_10_.refs_26_), channel_id=1, source_target_pairs={{0,32},{16,48},{32,64},{48,80},{64,96},{80,112},{96,128},{112,144}... | collective-permute-start | bytes 811016 | tf_op jit(solution)/shard_map/spread_sums/ppermute | solution.py:546
  201.0 9.0 %collective-permute-start.23 = (f32[528,128]{1,0:T(8,128)}, f32[528,128]{1,0:T(8,128)}, u32[]{:S(2)}, u32[]{:S(2)}) collective-permute-start(f32[528,128]{1,0:T(8,128)} %collective-permute-done.21.refs_13_.refs_29_), channel_id=1, source_target_pairs={{0,224},{16,240},{32,0},{48,16},{64,32},{80,48},{96,64},{112,80},{... | collective-permute-start | bytes 811016 | tf_op jit(solution)/shard_map/spread_sums/ppermute | solution.py:549
  (25 other events, 102.9 us)
